TPU v7x, 512 devices: a whole 4x8x8 slice. The times are simulated.
512 devices in a mesh: section: 2 (over x_hi), lat: 16 (over x_lo, y), lon: 16 (over z, core).
Axes of the slice: x: 4 (x_hi: 2, x_lo: 2; x = x_hi * 2 + x_lo), y: 8, z: 8, core: 2. Of those that a mesh axis runs over, the one named last changes fastest.
Arguments:
- fields_in: bfloat16 [4, 96, 256, 2048], P('section', None, 'lat', 'lon'), may hold values from -6 to 6
- plan: int32 [4], replicated, may hold values from 0 to 3, as said below
- in_proj: bfloat16 [64, 96], replicated, may hold values from -0.625 to 0.625
- enc_conv: bfloat16 [9, 64, 64], replicated, may hold values from -0.25 to 0.25
- down_conv: bfloat16 [9, 128, 64], replicated, may hold values from -0.25 to 0.25
- mid_conv: bfloat16 [9, 128, 128], replicated, may hold values from -0.1875 to 0.1875
- up_proj: bfloat16 [64, 128], replicated, may hold values from -0.5 to 0.5
- unite_conv: bfloat16 [9, 64, 128], replicated, may hold values from -0.1875 to 0.1875
- out_proj: bfloat16 [96, 64], replicated, may hold values from -0.75 to 0.75
Outputs:
- corrected: bfloat16 [4, 96, 256, 2048], P('section', None, 'lat', 'lon')
Inputs may be any that keep to these rules, and one draw needn't show every extreme that they name: `plan`: each micro-batch appears once; the first turn takes one of the last 2 micro-batches and the last turn one of the first 2.
All inputs are finite; a program needn't handle non-finite values.
Results may differ from a plain program's by a relative error of at most 0.0072.
Values may be sent and summed in bfloat16 or wider, within the bound.
A program may use at most 64 MiB of HBM per device.

v0:
```python
import jax
import jax.numpy as jnp
from jax import lax
from jax.sharding import PartitionSpec as P


def padded_2(block, sides, width, periodic):
    for axis, dim in sides:
        count = lax.axis_size(axis)
        forward = [(i, i + 1) for i in range(count - 1)]
        if periodic:
            forward.append((count - 1, 0))
        backward = [(target, source) for source, target in forward]
        low = lax.ppermute(
            lax.slice_in_dim(block, block.shape[dim] - width, None, axis=dim), axis, forward
        )
        high = lax.ppermute(lax.slice_in_dim(block, 0, width, axis=dim), axis, backward)
        block = jnp.concatenate([low, block, high], axis=dim)
    return block


def copy_for_each(array, axis):
    size = lax.axis_size(axis)
    return lax.all_to_all(
        jnp.broadcast_to(array[None], (size, *array.shape)), axis, 0, 0, tiled=True
    )


def laid_out(pieces, dim):
    lengths = list(pieces.shape[1:])
    lengths[dim] *= pieces.shape[0]
    return jnp.moveaxis(pieces, 0, dim).reshape(lengths)


def gathered_copies(array, axis, dim):
    pieces = copy_for_each(array, axis)
    return laid_out(pieces, dim)


def convolve(source, kernel):
    batch, channels, height, breadth = source.shape
    tall = padded_2(source, (("lat", 2),), 1, False)
    padded = padded_2(tall, (("lon", 3),), 1, True)
    summed = jnp.zeros((batch, kernel.shape[1], height, breadth), jnp.float32)
    for offset_row in range(3):
        for offset_col in range(3):
            window = padded[
                :, :, offset_row : offset_row + height, offset_col : offset_col + breadth
            ]
            summed = summed + jnp.einsum(
                "oc,bchw->bohw",
                kernel[3 * offset_row + offset_col],
                window,
                preferred_element_type=jnp.float32,
            )
    return summed


def encode(sample, in_proj, enc_conv, down_conv):
    batch, variables, height, breadth = sample.shape
    stem_map = jax.nn.gelu(
        jnp.einsum("cv,bvhw->bchw", in_proj, sample, preferred_element_type=jnp.float32)
    )
    stem_map = stem_map.astype(jnp.bfloat16)
    skip_map = jax.nn.gelu(convolve(stem_map, enc_conv)).astype(jnp.bfloat16)
    pooled = (
        skip_map.astype(jnp.float32)
        .reshape(batch, -1, height // 2, 2, breadth // 2, 2)
        .mean(axis=(3, 5))
        .astype(jnp.bfloat16)
    )
    deep_map = jax.nn.gelu(convolve(pooled, down_conv)).astype(jnp.bfloat16)
    return (skip_map, deep_map)


def decode(skip_map, deep_map, mid_conv, up_proj, unite_conv, out_proj):
    middle = (jax.nn.gelu(convolve(deep_map, mid_conv)) + deep_map.astype(jnp.float32)).astype(
        jnp.bfloat16
    )
    lifted = jnp.einsum(
        "oc,bchw->bohw", up_proj, middle, preferred_element_type=jnp.float32
    ).astype(jnp.bfloat16)
    enlarged = jnp.repeat(jnp.repeat(lifted, 2, axis=2), 2, axis=3)
    joined = jnp.concatenate([enlarged, skip_map], axis=1)
    merged = jax.nn.gelu(convolve(joined, unite_conv)).astype(jnp.bfloat16)
    result = jnp.einsum("oc,bchw->bohw", out_proj, merged, preferred_element_type=jnp.float32)
    return result.astype(jnp.bfloat16)


def shards(fields_in, plan, in_proj, enc_conv, down_conv, mid_conv, up_proj, unite_conv, out_proj):
    per_section = fields_in.shape[0]
    section_index = lax.axis_index("section")
    gathered = gathered_copies(fields_in, "section", 0)
    picked = []
    for local_num in range(per_section):
        tick_num = section_index * per_section + local_num
        picked.append(lax.dynamic_index_in_dim(gathered, plan[tick_num], 0, keepdims=True))
    samples = jnp.concatenate(picked, axis=0)
    skip_map, deep_map = encode(samples, in_proj, enc_conv, down_conv)
    return decode(skip_map, deep_map, mid_conv, up_proj, unite_conv, out_proj)


def solution(mesh):
    return jax.shard_map(
        shards,
        mesh=mesh,
        in_specs=(P("section", None, "lat", "lon"), P(), P(), P(), P(), P(), P(), P(), P()),
        out_specs=P("section", None, "lat", "lon"),
        check_vma=False,
    )
```

profile of v0, /device:TPU:56, one launch (start us, length us, event | category | flops | bytes accessed | tf_op | source)
XLA Modules:
  0.0 122.0 jit_solution(8548886672546733544)
XLA Ops:
  0.0 1.3 %copy.18 = bf16[2,96,16,128]{3,1,2,0:T(8,128)(2,1)S(1)} copy(bf16[2,96,16,128]{3,2,1,0:T(8,128)(2,1)} %param.9) | data formatting | bytes 1572864 | tf_op args[0]
  1.4 1.4 %broadcast_in_dim.12 = bf16[2,2,96,16,128]{4,2,3,1,0:T(8,128)(2,1)} broadcast(bf16[2,96,16,128]{3,1,2,0:T(8,128)(2,1)S(1)} %copy.18), dimensions={1,2,3,4} | broadcast | bytes 2359296 | tf_op jit(solution)/shard_map/broadcast_in_dim | solution.py:25
  2.8 4.4 %all-to-all-start = ((bf16[2,2,96,16,128]{4,2,3,1,0:T(8,128)(2,1)}), bf16[2,2,96,16,128]{4,2,3,1,0:T(8,128)(2,1)S(1)}, u32[]{:S(2)}, u32[]{:S(2)}) async-start(bf16[2,2,96,16,128]{4,2,3,1,0:T(8,128)(2,1)} %broadcast_in_dim.12), calls=%async_computation | async-start | bytes 3145728 | tf_op jit(solution)/shard_map/all_to_all | solution.py:24
  7.2 0.7 fusion.248
  11.7 16.2 %all-to-all-done = bf16[2,2,96,16,128]{4,2,3,1,0:T(8,128)(2,1)S(1)} async-done(((bf16[2,2,96,16,128]{4,2,3,1,0:T(8,128)(2,1)}), bf16[2,2,96,16,128]{4,2,3,1,0:T(8,128)(2,1)S(1)}, u32[]{:S(2)}, u32[]{:S(2)}) %all-to-all-start) | async-done | bytes 1572896 | tf_op jit(solution)/shard_map/all_to_all | solution.py:24
  28.0 0.5 fusion.32
  28.5 2.3 %collective-permute-start = (bf16[2,64,1,128]{3,1,2,0:T(8,128)(2,1)S(1)}, bf16[2,64,1,128]{3,1,2,0:T(8,128)(2,1)S(1)}, u32[]{:S(2)}, u32[]{:S(2)}) collective-permute-start(bf16[2,64,1,128]{3,1,2,0:T(8,128)(2,1)S(1)} %get-tuple-element.17), channel_id=1, source_target_pairs={{0,16},{16,32},{32,48},{48,64},{64,80},{80,96},{96,112},{112,128},... | collective-permute-start | bytes 98312 | tf_op jit(solution)/shard_map/ppermute | solution.py:14
  30.8 3.7 %collective-permute-start.1 = (bf16[2,64,1,128]{3,1,2,0:T(8,128)(2,1)S(1)}, bf16[2,64,1,128]{3,1,2,0:T(8,128)(2,1)S(1)}, u32[]{:S(2)}, u32[]{:S(2)}) collective-permute-start(bf16[2,64,1,128]{3,1,2,0:T(8,128)(2,1)S(1)} %get-tuple-element.18), channel_id=1, source_target_pairs={{16,0},{32,16},{48,32},{64,48},{80,64},{96,80},{112,96},{128,112},... | collective-permute-start | bytes 98312 | tf_op jit(solution)/shard_map/ppermute | solution.py:17
  34.5 4.3 %collective-permute-done.1 = bf16[2,64,1,128]{3,1,2,0:T(8,128)(2,1)S(1)} collective-permute-done((bf16[2,64,1,128]{3,1,2,0:T(8,128)(2,1)S(1)}, bf16[2,64,1,128]{3,1,2,0:T(8,128)(2,1)S(1)}, u32[]{:S(2)}, u32[]{:S(2)}) %collective-permute-start.1) | collective-permute-done | bytes 32800 | tf_op jit(solution)/shard_map/ppermute | solution.py:17
  39.8 6.2 %collective-permute-start.3 = (bf16[2,64,18,1]{1,0,3,2:T(2,128)(2,1)S(1)}, bf16[2,64,18,1]{1,0,3,2:T(2,128)(2,1)S(1)}, u32[]{:S(2)}, u32[]{:S(2)}) collective-permute-start(bf16[2,64,18,1]{1,0,3,2:T(2,128)(2,1)S(1)} %copy.21), channel_id=1, source_target_pairs={{1,0},{2,1},{3,2},{4,3},{5,4},{6,5},{7,6},{8,7},{9,8},{10,9},{11,1... | collective-permute-start | bytes 13832 | tf_op jit(solution)/shard_map/ppermute | solution.py:17
  46.3 0.8 collective-permute-done.2
  47.0 0.4 copy.20
  47.4 0.4 copy.22
  47.8 0.8 maximum_maximum_fusion.1
  51.0 0.6 fusion.40
  51.9 1.7 %reduce_sum.9 = f32[2,64,8,64]{1,3,2,0:T(8,128)S(1)} reduce(f32[2,64,8,2,64,2]{1,5,4,3,2,0:T(2,128)S(1)} %bitcast.318, f32[]{:T(128)} %constant.37.clone.1), dimensions={3,5}, to_apply=%region_0.1 | reduce | flops 196608 | bytes 1310724 | tf_op jit(solution)/shard_map/reduce_sum | solution.py:69
  53.7 1.9 %collective-permute-start.4 = (bf16[2,64,1,64]{1,3,2,0:T(8,128)(2,1)S(1)}, bf16[2,64,1,64]{1,3,2,0:T(8,128)(2,1)S(1)}, u32[]{:S(2)}, u32[]{:S(2)}) collective-permute-start(bf16[2,64,1,64]{1,3,2,0:T(8,128)(2,1)S(1)} %get-tuple-element.29), channel_id=1, source_target_pairs={{0,16},{16,32},{32,48},{48,64},{64,80},{80,96},{96,112},{112,128},... | collective-permute-start | bytes 49160 | tf_op jit(solution)/shard_map/ppermute | solution.py:14
  55.6 3.9 %collective-permute-start.5 = (bf16[2,64,1,64]{1,3,2,0:T(8,128)(2,1)S(1)}, bf16[2,64,1,64]{1,3,2,0:T(8,128)(2,1)S(1)}, u32[]{:S(2)}, u32[]{:S(2)}) collective-permute-start(bf16[2,64,1,64]{1,3,2,0:T(8,128)(2,1)S(1)} %get-tuple-element.30), channel_id=1, source_target_pairs={{16,0},{32,16},{48,32},{64,48},{80,64},{96,80},{112,96},{128,112},... | collective-permute-start | bytes 49160 | tf_op jit(solution)/shard_map/ppermute | solution.py:17
  59.7 3.8 %collective-permute-done.5 = bf16[2,64,1,64]{1,3,2,0:T(8,128)(2,1)S(1)} collective-permute-done((bf16[2,64,1,64]{1,3,2,0:T(8,128)(2,1)S(1)}, bf16[2,64,1,64]{1,3,2,0:T(8,128)(2,1)S(1)}, u32[]{:S(2)}, u32[]{:S(2)}) %collective-permute-start.5) | collective-permute-done | bytes 16416 | tf_op jit(solution)/shard_map/ppermute | solution.py:17
  63.6 2.9 %collective-permute-start.7 = (bf16[2,64,10,1]{1,3,2,0:T(2,128)(2,1)S(1)}, bf16[2,64,10,1]{1,3,2,0:T(2,128)(2,1)S(1)}, u32[]{:S(2)}, u32[]{:S(2)}) collective-permute-start(bf16[2,64,10,1]{1,3,2,0:T(2,128)(2,1)S(1)} %get-tuple-element.26), channel_id=1, source_target_pairs={{1,0},{2,1},{3,2},{4,3},{5,4},{6,5},{7,6},{8,7},{9,8},{10,9},{11,1... | collective-permute-start | bytes 7688 | tf_op jit(solution)/shard_map/ppermute | solution.py:17
  66.9 0.9 collective-permute-done.6
  69.1 0.4 fusion.78
  69.5 1.9 %collective-permute-start.8 = (bf16[2,128,1,64]{1,3,2,0:T(8,128)(2,1)S(1)}, bf16[2,128,1,64]{1,3,2,0:T(8,128)(2,1)S(1)}, u32[]{:S(2)}, u32[]{:S(2)}) collective-permute-start(bf16[2,128,1,64]{1,3,2,0:T(8,128)(2,1)S(1)} %get-tuple-element.27), channel_id=1, source_target_pairs={{0,16},{16,32},{32,48},{48,64},{64,80},{80,96},{96,112},{112,128},... | collective-permute-start | bytes 98312 | tf_op jit(solution)/shard_map/ppermute | solution.py:14
  71.5 4.1 %collective-permute-start.9 = (bf16[2,128,1,64]{1,3,2,0:T(8,128)(2,1)S(1)}, bf16[2,128,1,64]{1,3,2,0:T(8,128)(2,1)S(1)}, u32[]{:S(2)}, u32[]{:S(2)}) collective-permute-start(bf16[2,128,1,64]{1,3,2,0:T(8,128)(2,1)S(1)} %get-tuple-element.28), channel_id=1, source_target_pairs={{16,0},{32,16},{48,32},{64,48},{80,64},{96,80},{112,96},{128,112},... | collective-permute-start | bytes 98312 | tf_op jit(solution)/shard_map/ppermute | solution.py:17
  75.8 3.6 %collective-permute-done.9 = bf16[2,128,1,64]{1,3,2,0:T(8,128)(2,1)S(1)} collective-permute-done((bf16[2,128,1,64]{1,3,2,0:T(8,128)(2,1)S(1)}, bf16[2,128,1,64]{1,3,2,0:T(8,128)(2,1)S(1)}, u32[]{:S(2)}, u32[]{:S(2)}) %collective-permute-start.9) | collective-permute-done | bytes 32800 | tf_op jit(solution)/shard_map/ppermute | solution.py:17
  79.4 2.9 %collective-permute-start.11 = (bf16[2,128,10,1]{1,3,2,0:T(2,128)(2,1)S(1)}, bf16[2,128,10,1]{1,3,2,0:T(2,128)(2,1)S(1)}, u32[]{:S(2)}, u32[]{:S(2)}) collective-permute-start(bf16[2,128,10,1]{1,3,2,0:T(2,128)(2,1)S(1)} %get-tuple-element.22), channel_id=1, source_target_pairs={{1,0},{2,1},{3,2},{4,3},{5,4},{6,5},{7,6},{8,7},{9,8},{10,9},{11,1... | collective-permute-start | bytes 15368 | tf_op jit(solution)/shard_map/ppermute | solution.py:17
  82.8 0.9 collective-permute-done.10
  85.2 1.3 %fusion.24 = bf16[2,64,8,64]{1,3,2,0:T(8,128)(2,1)S(1)} fusion(f32[2,8,64,128]{3,2,1,0:T(8,128)S(1)} %fusion.119, f32[2,8,64,128]{3,2,1,0:T(8,128)S(1)} %fusion.115, f32[2,8,64,128]{3,2,1,0:T(8,128)S(1)} %fusion.121, f32[2,8,64,128]{3,2,1,0:T(8,128)S(1)} %fusion.19, bf16[2,128,8,64]{1,3,2,0:T(8,128)(2,1)S(1)} %fusion.78, ...), kind=kOutput, calls=%fused_computation.48 | convolution fusion | flops 52363264 | bytes 2801664 | tf_op jit(solution)/shard_map/oc,bchw->bohw/dot_general | solution.py:80
  87.2 0.9 copy.25
  88.1 2.3 %collective-permute-start.12 = (bf16[2,128,1,128]{3,1,2,0:T(8,128)(2,1)S(1)}, bf16[2,128,1,128]{3,1,2,0:T(8,128)(2,1)S(1)}, u32[]{:S(2)}, u32[]{:S(2)}) collective-permute-start(bf16[2,128,1,128]{3,1,2,0:T(8,128)(2,1)S(1)} %get-tuple-element.11), channel_id=1, source_target_pairs={{0,16},{16,32},{32,48},{48,64},{64,80},{80,96},{96,112},{112,128},... | collective-permute-start | bytes 196616 | tf_op jit(solution)/shard_map/ppermute | solution.py:14
  90.4 3.5 %collective-permute-start.13 = (bf16[2,128,1,128]{3,1,2,0:T(8,128)(2,1)S(1)}, bf16[2,128,1,128]{3,1,2,0:T(8,128)(2,1)S(1)}, u32[]{:S(2)}, u32[]{:S(2)}) collective-permute-start(bf16[2,128,1,128]{3,1,2,0:T(8,128)(2,1)S(1)} %get-tuple-element.12), channel_id=1, source_target_pairs={{16,0},{32,16},{48,32},{64,48},{80,64},{96,80},{112,96},{128,112},... | collective-permute-start | bytes 196616 | tf_op jit(solution)/shard_map/ppermute | solution.py:17
  94.0 2.0 %fusion.64 = f32[2,16,128,64]{2,3,1,0:T(8,128)} fusion(bf16[2,64,16,128]{3,1,2,0:T(8,128)(2,1)S(1)} %fusion.40, bf16[2,64,16,128]{3,1,2,0:T(8,128)(2,1)S(1)} %copy.25, bf16[9,64,128]{2,1,0:T(8,128)(2,1)} %param.16), kind=kOutput, calls=%fused_computation.91 | convolution fusion | flops 69206016 | bytes 2113536 | tf_op jit(solution)/shard_map/oc,bchw->bohw/dot_general | solution.py:50
  96.0 2.7 %collective-permute-done.13 = bf16[2,128,1,128]{3,1,2,0:T(8,128)(2,1)S(1)} collective-permute-done((bf16[2,128,1,128]{3,1,2,0:T(8,128)(2,1)S(1)}, bf16[2,128,1,128]{3,1,2,0:T(8,128)(2,1)S(1)}, u32[]{:S(2)}, u32[]{:S(2)}) %collective-permute-start.13) | collective-permute-done | bytes 65568 | tf_op jit(solution)/shard_map/ppermute | solution.py:17
  98.8 0.5 fusion.243
  99.3 1.0 copy.26
  100.4 0.4 copy.28
  100.8 3.0 %collective-permute-start.15 = (bf16[2,128,18,1]{1,0,3,2:T(2,128)(2,1)S(1)}, bf16[2,128,18,1]{1,0,3,2:T(2,128)(2,1)}, u32[]{:S(2)}, u32[]{:S(2)}) collective-permute-start(bf16[2,128,18,1]{1,0,3,2:T(2,128)(2,1)S(1)} %copy.28), channel_id=1, source_target_pairs={{1,0},{2,1},{3,2},{4,3},{5,4},{6,5},{7,6},{8,7},{9,8},{10,9},{11,1... | collective-permute-start | bytes 27656 | tf_op jit(solution)/shard_map/ppermute | solution.py:17
  103.7 2.0 %fusion.61 = f32[2,16,128,64]{2,3,1,0:T(8,128)} fusion(bf16[2,128,1,128]{3,1,2,0:T(8,128)(2,1)S(1)} %collective-permute-done.12, bf16[2,64,16,128]{3,1,2,0:T(8,128)(2,1)S(1)} %fusion.40, bf16[2,64,16,128]{3,1,2,0:T(8,128)(2,1)S(1)} %copy.25, bf16[9,64,128]{2,1,0:T(8,128)(2,1)} %param.16), kind=kOutput, calls=%fused_computation.87 | convolution fusion | flops 70254592 | bytes 2179072 | tf_op jit(solution)/shard_map/oc,bchw->bohw/dot_general | solution.py:50
  105.7 2.0 %fusion.51 = f32[2,16,128,64]{2,3,1,0:T(8,128)} fusion(bf16[2,128,1,128]{3,1,2,0:T(8,128)(2,1)S(1)} %collective-permute-done.13, bf16[2,64,16,128]{3,1,2,0:T(8,128)(2,1)S(1)} %fusion.40, bf16[2,64,16,128]{3,1,2,0:T(8,128)(2,1)S(1)} %copy.25, bf16[9,64,128]{2,1,0:T(8,128)(2,1)} %param.16), kind=kOutput, calls=%fused_computation.76 | convolution fusion | flops 70254592 | bytes 2179072 | tf_op jit(solution)/shard_map/oc,bchw->bohw/dot_general | solution.py:50
  107.7 0.6 copy.27
  108.4 1.3 %copy.29 = bf16[2,128,18,1]{3,1,2,0:T(8,128)(2,1)S(1)} copy(bf16[2,128,18,1]{1,0,3,2:T(2,128)(2,1)} %collective-permute-done.15) | data formatting | bytes 18432 | tf_op jit(solution)/shard_map/ppermute | solution.py:17
  109.7 2.8 %maximum_maximum_fusion = (bf16[2,128,18,129]{3,1,2,0:T(8,128)(2,1)S(1)}, bf16[2,128,18,129]{3,1,2,0:T(8,128)(2,1)S(1)}) fusion(bf16[2,128,1,128]{3,1,2,0:T(8,128)(2,1)S(1)} %collective-permute-done.13, bf16[2,64,16,128]{3,1,2,0:T(8,128)(2,1)S(1)} %fusion.40, bf16[2,64,16,128]{3,1,2,0:T(8,128)(2,1)S(1)} %copy.25, ...), kind=kLoop, calls=%fused_computation | loop fusion | flops 11888640 | bytes 3575808 | tf_op jit(solution)/shard_map/concatenate | solution.py:18
  112.6 0.6 fusion.59
  113.2 0.6 fusion.49
  114.4 0.6 copy-done.2
  115.3 0.4 fusion.6
  115.7 4.0 %fusion.9 = bf16[2,96,16,128]{3,1,2,0:T(8,128)(2,1)} fusion(f32[2,16,128,64]{2,3,1,0:T(8,128)S(1)} %fusion.49, f32[2,16,128,64]{2,3,1,0:T(8,128)} %fusion.51, f32[2,16,128,64]{2,3,1,0:T(8,128)S(1)} %fusion.53, f32[2,16,128,64]{2,3,1,0:T(8,128)S(1)} %fusion.6, bf16[2,128,18,129]{3,1,2,0:T(8,128)(2,1)} %copy-done.1, bf16[96,64]{0,1:T(8,128)(2,1)S(1)} %copy-done, ...), kind=kOutput, calls=%fused_computation.25 | convolution fusion | flops 121241600 | bytes 6057984 | tf_op jit(solution)/shard_map/oc,bchw->bohw/dot_general | solution.py:86
  119.7 2.3 %copy.30 = bf16[2,96,16,128]{3,2,1,0:T(8,128)(2,1)} copy(bf16[2,96,16,128]{3,1,2,0:T(8,128)(2,1)} %fusion.9) | data formatting | bytes 1572864 | tf_op jit(solution)/shard_map/convert_element_type | solution.py:87
  (79 shorter events, 9.6 us)
Async XLA Ops:
  0.0 115.7 %copy-start = (bf16[96,64]{0,1:T(8,128)(2,1)S(1)}, bf16[96,64]{0,1:T(8,128)(2,1)}, u32[]{:S(2)}) copy-start(bf16[96,64]{0,1:T(8,128)(2,1)} %param.17) | copy-start | bytes 36868
  1.4 5.9 %copy-start.9 = (s32[4]{0:T(128)S(1)}, s32[4]{0:T(128)}, u32[]{:S(2)}) copy-start(s32[4]{0:T(128)} %param.10) | copy-start | bytes 52
  2.8 25.2 %copy-start.10 = (bf16[64,96]{1,0:T(8,128)(2,1)S(1)}, bf16[64,96]{1,0:T(8,128)(2,1)}, u32[]{:S(2)}) copy-start(bf16[64,96]{1,0:T(8,128)(2,1)} %param.11) | copy-start | bytes 36868
  2.8 25.1 %all-to-all-start = ((bf16[2,2,96,16,128]{4,2,3,1,0:T(8,128)(2,1)}), bf16[2,2,96,16,128]{4,2,3,1,0:T(8,128)(2,1)S(1)}, u32[]{:S(2)}, u32[]{:S(2)}) async-start(bf16[2,2,96,16,128]{4,2,3,1,0:T(8,128)(2,1)} %broadcast_in_dim.12), calls=%async_computation | async-start | bytes 3145728 | tf_op jit(solution)/shard_map/all_to_all | solution.py:24
  28.5 6.0 %collective-permute-start = (bf16[2,64,1,128]{3,1,2,0:T(8,128)(2,1)S(1)}, bf16[2,64,1,128]{3,1,2,0:T(8,128)(2,1)S(1)}, u32[]{:S(2)}, u32[]{:S(2)}) collective-permute-start(bf16[2,64,1,128]{3,1,2,0:T(8,128)(2,1)S(1)} %get-tuple-element.17), channel_id=1, source_target_pairs={{0,16},{16,32},{32,48},{48,64},{64,80},{80,96},{96,112},{112,128},... | collective-permute-start | bytes 98312 | tf_op jit(solution)/shard_map/ppermute | solution.py:14
  30.8 15.2 %copy-start.6 = (bf16[9,64,64]{2,1,0:T(8,128)(2,1)S(1)}, bf16[9,64,64]{2,1,0:T(8,128)(2,1)}, u32[]{:S(2)}) copy-start(bf16[9,64,64]{2,1,0:T(8,128)(2,1)} %param.12) | copy-start | bytes 221188
  30.8 8.0 %collective-permute-start.1 = (bf16[2,64,1,128]{3,1,2,0:T(8,128)(2,1)S(1)}, bf16[2,64,1,128]{3,1,2,0:T(8,128)(2,1)S(1)}, u32[]{:S(2)}, u32[]{:S(2)}) collective-permute-start(bf16[2,64,1,128]{3,1,2,0:T(8,128)(2,1)S(1)} %get-tuple-element.18), channel_id=1, source_target_pairs={{16,0},{32,16},{48,32},{64,48},{80,64},{96,80},{112,96},{128,112},... | collective-permute-start | bytes 98312 | tf_op jit(solution)/shard_map/ppermute | solution.py:17
  39.5 7.5 %collective-permute-start.2 = (bf16[2,64,18,1]{1,0,3,2:T(2,128)(2,1)S(1)}, bf16[2,64,18,1]{1,0,3,2:T(2,128)(2,1)S(1)}, u32[]{:S(2)}, u32[]{:S(2)}) collective-permute-start(bf16[2,64,18,1]{1,0,3,2:T(2,128)(2,1)S(1)} %copy.19), channel_id=1, source_target_pairs={{0,1},{1,2},{2,3},{3,4},{4,5},{5,6},{6,7},{7,8},{8,9},{9,10},{10,1... | collective-permute-start | bytes 13832 | tf_op jit(solution)/shard_map/ppermute | solution.py:14
  39.8 7.6 %collective-permute-start.3 = (bf16[2,64,18,1]{1,0,3,2:T(2,128)(2,1)S(1)}, bf16[2,64,18,1]{1,0,3,2:T(2,128)(2,1)S(1)}, u32[]{:S(2)}, u32[]{:S(2)}) collective-permute-start(bf16[2,64,18,1]{1,0,3,2:T(2,128)(2,1)S(1)} %copy.21), channel_id=1, source_target_pairs={{1,0},{2,1},{3,2},{4,3},{5,4},{6,5},{7,6},{8,7},{9,8},{10,9},{11,1... | collective-permute-start | bytes 13832 | tf_op jit(solution)/shard_map/ppermute | solution.py:17
  51.9 7.7 %copy-start.5 = (bf16[9,128,64]{1,2,0:T(8,128)(2,1)S(1)}, bf16[9,128,64]{1,2,0:T(8,128)(2,1)}, u32[]{:S(2)}) copy-start(bf16[9,128,64]{1,2,0:T(8,128)(2,1)} %param.13) | copy-start | bytes 442372
  53.7 6.1 %collective-permute-start.4 = (bf16[2,64,1,64]{1,3,2,0:T(8,128)(2,1)S(1)}, bf16[2,64,1,64]{1,3,2,0:T(8,128)(2,1)S(1)}, u32[]{:S(2)}, u32[]{:S(2)}) collective-permute-start(bf16[2,64,1,64]{1,3,2,0:T(8,128)(2,1)S(1)} %get-tuple-element.29), channel_id=1, source_target_pairs={{0,16},{16,32},{32,48},{48,64},{64,80},{80,96},{96,112},{112,128},... | collective-permute-start | bytes 49160 | tf_op jit(solution)/shard_map/ppermute | solution.py:14
  55.6 7.9 %collective-permute-start.5 = (bf16[2,64,1,64]{1,3,2,0:T(8,128)(2,1)S(1)}, bf16[2,64,1,64]{1,3,2,0:T(8,128)(2,1)S(1)}, u32[]{:S(2)}, u32[]{:S(2)}) collective-permute-start(bf16[2,64,1,64]{1,3,2,0:T(8,128)(2,1)S(1)} %get-tuple-element.30), channel_id=1, source_target_pairs={{16,0},{32,16},{48,32},{64,48},{80,64},{96,80},{112,96},{128,112},... | collective-permute-start | bytes 49160 | tf_op jit(solution)/shard_map/ppermute | solution.py:17
  63.5 4.3 %collective-permute-start.6 = (bf16[2,64,10,1]{1,3,2,0:T(2,128)(2,1)S(1)}, bf16[2,64,10,1]{1,3,2,0:T(2,128)(2,1)S(1)}, u32[]{:S(2)}, u32[]{:S(2)}) collective-permute-start(bf16[2,64,10,1]{1,3,2,0:T(2,128)(2,1)S(1)} %get-tuple-element.25), channel_id=1, source_target_pairs={{0,1},{1,2},{2,3},{3,4},{4,5},{5,6},{6,7},{7,8},{8,9},{9,10},{10,1... | collective-permute-start | bytes 7688 | tf_op jit(solution)/shard_map/ppermute | solution.py:14
  63.6 4.3 %collective-permute-start.7 = (bf16[2,64,10,1]{1,3,2,0:T(2,128)(2,1)S(1)}, bf16[2,64,10,1]{1,3,2,0:T(2,128)(2,1)S(1)}, u32[]{:S(2)}, u32[]{:S(2)}) collective-permute-start(bf16[2,64,10,1]{1,3,2,0:T(2,128)(2,1)S(1)} %get-tuple-element.26), channel_id=1, source_target_pairs={{1,0},{2,1},{3,2},{4,3},{5,4},{6,5},{7,6},{8,7},{9,8},{10,9},{11,1... | collective-permute-start | bytes 7688 | tf_op jit(solution)/shard_map/ppermute | solution.py:17
  68.9 6.7 %copy-start.4 = (bf16[9,128,128]{2,1,0:T(8,128)(2,1)S(1)}, bf16[9,128,128]{2,1,0:T(8,128)(2,1)}, u32[]{:S(2)}) copy-start(bf16[9,128,128]{2,1,0:T(8,128)(2,1)} %param.14) | copy-start | bytes 884740
  69.5 6.3 %collective-permute-start.8 = (bf16[2,128,1,64]{1,3,2,0:T(8,128)(2,1)S(1)}, bf16[2,128,1,64]{1,3,2,0:T(8,128)(2,1)S(1)}, u32[]{:S(2)}, u32[]{:S(2)}) collective-permute-start(bf16[2,128,1,64]{1,3,2,0:T(8,128)(2,1)S(1)} %get-tuple-element.27), channel_id=1, source_target_pairs={{0,16},{16,32},{32,48},{48,64},{64,80},{80,96},{96,112},{112,128},... | collective-permute-start | bytes 98312 | tf_op jit(solution)/shard_map/ppermute | solution.py:14
  71.5 7.9 %collective-permute-start.9 = (bf16[2,128,1,64]{1,3,2,0:T(8,128)(2,1)S(1)}, bf16[2,128,1,64]{1,3,2,0:T(8,128)(2,1)S(1)}, u32[]{:S(2)}, u32[]{:S(2)}) collective-permute-start(bf16[2,128,1,64]{1,3,2,0:T(8,128)(2,1)S(1)} %get-tuple-element.28), channel_id=1, source_target_pairs={{16,0},{32,16},{48,32},{64,48},{80,64},{96,80},{112,96},{128,112},... | collective-permute-start | bytes 98312 | tf_op jit(solution)/shard_map/ppermute | solution.py:17
  79.4 4.3 %collective-permute-start.10 = (bf16[2,128,10,1]{1,3,2,0:T(2,128)(2,1)S(1)}, bf16[2,128,10,1]{1,3,2,0:T(2,128)(2,1)S(1)}, u32[]{:S(2)}, u32[]{:S(2)}) collective-permute-start(bf16[2,128,10,1]{1,3,2,0:T(2,128)(2,1)S(1)} %get-tuple-element.21), channel_id=1, source_target_pairs={{0,1},{1,2},{2,3},{3,4},{4,5},{5,6},{6,7},{7,8},{8,9},{9,10},{10,1... | collective-permute-start | bytes 15368 | tf_op jit(solution)/shard_map/ppermute | solution.py:14
  79.4 4.3 %collective-permute-start.11 = (bf16[2,128,10,1]{1,3,2,0:T(2,128)(2,1)S(1)}, bf16[2,128,10,1]{1,3,2,0:T(2,128)(2,1)S(1)}, u32[]{:S(2)}, u32[]{:S(2)}) collective-permute-start(bf16[2,128,10,1]{1,3,2,0:T(2,128)(2,1)S(1)} %get-tuple-element.22), channel_id=1, source_target_pairs={{1,0},{2,1},{3,2},{4,3},{5,4},{6,5},{7,6},{8,7},{9,8},{10,9},{11,1... | collective-permute-start | bytes 15368 | tf_op jit(solution)/shard_map/ppermute | solution.py:17
  84.4 0.8 copy-start.8
  88.1 7.9 %collective-permute-start.12 = (bf16[2,128,1,128]{3,1,2,0:T(8,128)(2,1)S(1)}, bf16[2,128,1,128]{3,1,2,0:T(8,128)(2,1)S(1)}, u32[]{:S(2)}, u32[]{:S(2)}) collective-permute-start(bf16[2,128,1,128]{3,1,2,0:T(8,128)(2,1)S(1)} %get-tuple-element.11), channel_id=1, source_target_pairs={{0,16},{16,32},{32,48},{48,64},{64,80},{80,96},{96,112},{112,128},... | collective-permute-start | bytes 196616 | tf_op jit(solution)/shard_map/ppermute | solution.py:14
  90.4 8.3 %collective-permute-start.13 = (bf16[2,128,1,128]{3,1,2,0:T(8,128)(2,1)S(1)}, bf16[2,128,1,128]{3,1,2,0:T(8,128)(2,1)S(1)}, u32[]{:S(2)}, u32[]{:S(2)}) collective-permute-start(bf16[2,128,1,128]{3,1,2,0:T(8,128)(2,1)S(1)} %get-tuple-element.12), channel_id=1, source_target_pairs={{16,0},{32,16},{48,32},{64,48},{80,64},{96,80},{112,96},{128,112},... | collective-permute-start | bytes 196616 | tf_op jit(solution)/shard_map/ppermute | solution.py:17
  100.3 7.4 %collective-permute-start.14 = (bf16[2,128,18,1]{1,0,3,2:T(2,128)(2,1)}, bf16[2,128,18,1]{1,0,3,2:T(2,128)(2,1)S(1)}, u32[]{:S(2)}, u32[]{:S(2)}) collective-permute-start(bf16[2,128,18,1]{1,0,3,2:T(2,128)(2,1)} %copy.26), channel_id=1, source_target_pairs={{0,1},{1,2},{2,3},{3,4},{4,5},{5,6},{6,7},{7,8},{8,9},{9,10},{10,1... | collective-permute-start | bytes 27656 | tf_op jit(solution)/shard_map/ppermute | solution.py:14
  100.8 7.6 %collective-permute-start.15 = (bf16[2,128,18,1]{1,0,3,2:T(2,128)(2,1)S(1)}, bf16[2,128,18,1]{1,0,3,2:T(2,128)(2,1)}, u32[]{:S(2)}, u32[]{:S(2)}) collective-permute-start(bf16[2,128,18,1]{1,0,3,2:T(2,128)(2,1)S(1)} %copy.28), channel_id=1, source_target_pairs={{1,0},{2,1},{3,2},{4,3},{5,4},{6,5},{7,6},{8,7},{9,8},{10,9},{11,1... | collective-permute-start | bytes 27656 | tf_op jit(solution)/shard_map/ppermute | solution.py:17
  109.7 2.9 %copy-start.7 = (bf16[9,64,128]{2,1,0:T(8,128)(2,1)S(1)}, bf16[9,64,128]{2,1,0:T(8,128)(2,1)}, u32[]{:S(2)}) copy-start(bf16[9,64,128]{2,1,0:T(8,128)(2,1)} %param.16) | copy-start | bytes 442372
  112.6 1.5 %copy-start.1 = (bf16[2,128,18,129]{3,1,2,0:T(8,128)(2,1)}, bf16[2,128,18,129]{3,1,2,0:T(8,128)(2,1)S(1)}, u32[]{:S(2)}) copy-start(bf16[2,128,18,129]{3,1,2,0:T(8,128)(2,1)S(1)} %get-tuple-element.8) | copy-start | bytes 3566596
  113.7 1.2 %copy-start.2 = (f32[2,16,128,64]{2,3,1,0:T(8,128)S(1)}, f32[2,16,128,64]{2,3,1,0:T(8,128)}, u32[]{:S(2)}) copy-start(f32[2,16,128,64]{2,3,1,0:T(8,128)} %fusion.64) | copy-start | bytes 3145732
  113.7 1.5 %copy-start.3 = (f32[2,16,128,64]{2,3,1,0:T(8,128)S(1)}, f32[2,16,128,64]{2,3,1,0:T(8,128)}, u32[]{:S(2)}) copy-start(f32[2,16,128,64]{2,3,1,0:T(8,128)} %fusion.61) | copy-start | bytes 3145732
where the time goes:
time: 123 us; the launch traced here: 122 us
  starting transfers between devices  43.2 us (35%)
  waiting for transfers between devices  33.2 us (27%)
  matrix products  20.8 us (17%)
  local copies, waits for them, and re-layouts  14.3 us (12%)
  other arithmetic  5.99 us (5%)
  between operations  4.46 us (4%)
    ppermute x8, starting transfers between devices, padded_2(): lax.ppermute(lax.slice_in_dim(block, 0, width, axis=dim), axis, backward)  30.3 us
    all_to_all x1, waiting for transfers between devices, copy_for_each(): lax.all_to_all(jnp.broadcast_to(array[None], (size, *array.shape)), axis,...  16.2 us
    dot_general x34, matrix products, convolve(): jnp.einsum('oc,bchw->bohw', kernel[3 * offset_row + offset_col], window,...  15 us
    ppermute x8, waiting for transfers between devices, padded_2(): lax.ppermute(lax.slice_in_dim(block, 0, width, axis=dim), axis, backward)  14.4 us
    ppermute x8, starting transfers between devices, padded_2(): lax.ppermute(lax.slice_in_dim(block, block.shape[dim] - width, None, axis...  8.43 us
    all_to_all x1, starting transfers between devices, copy_for_each(): lax.all_to_all(jnp.broadcast_to(array[None], (size, *array.shape)), axis,...  4.42 us
    concatenate x6, other arithmetic, padded_2(): block = jnp.concatenate([low, block, high], axis=dim)  4.18 us
    dot_general x1, matrix products, decode(): jnp.einsum('oc,bchw->bohw', out_proj, merged, preferred_element_type=jnp....  4 us
  transfers between devices with their start and end apart: 17, of which 8 were waited for; matrix products, arithmetic and copies ran while one was open for 8% of the time, Pallas kernels for 0%

commit v1 on v0

v1 whole, which is shorter than its diff:
```python
import functools

import jax
import jax.numpy as jnp
from jax import lax
from jax.experimental import pallas as pl
from jax.experimental.pallas import tpu as pltpu
from jax.sharding import PartitionSpec as P

F32, BF = jnp.float32, jnp.bfloat16
MESH = pl.DeviceIdType.MESH

VARS, C0, C1 = 96, 64, 128
H, W = 16, 128
HP, WP = H // 2, W // 2
EXT = WP + 16
PADDED = EXT + 16
MID = slice(8, 8 + EXT)
PREV = slice(7, 7 + EXT)
NEXT = slice(9, 9 + EXT)
OWN = slice(16, 16 + WP)
OWN_PREV = slice(15, 15 + WP)
OWN_NEXT = slice(17, 17 + WP)


def gelu(x):
    half = 0.5 * x
    inner = x * (0.7978845608028654 + 0.035677408136300125 * (x * x))
    return half + half * jnp.tanh(inner)


def rounded(x):
    return x.astype(BF).astype(F32)


def nn(a, b):
    return jnp.dot(a, b, preferred_element_type=F32)


def nt(a, b):
    return lax.dot_general(a, b, (((1,), (1,)), ((), ())), preferred_element_type=F32)


def grid_iota(rows, cols):
    shape = (rows, cols)
    return lax.broadcasted_iota(jnp.int32, shape, 0), lax.broadcasted_iota(jnp.int32, shape, 1)


def one_hot(mask):
    return jnp.where(mask, 1.0, 0.0).astype(BF)


def eye(n):
    i, j = grid_iota(n, n)
    return one_hot(i == j)


def upper_lanes(rows):
    return lax.broadcasted_iota(jnp.int32, (rows, 128), 1) >= 64


def column_pairs(taps, channels):
    zero = jnp.zeros((C0, channels), BF)
    unit = eye(channels)
    out = []
    for a in range(3):
        b0, b1, b2 = taps[3 * a], taps[3 * a + 1], taps[3 * a + 2]
        stacked = jnp.concatenate([zero, b2, b1, b0, b2, b1, b0, zero], axis=0)
        out.append(nt(unit, stacked).astype(BF))
    return out


def fill_full_res(w_ref, base, blocks, rows):
    for k in range(4):
        for dr in range(2):
            a = k - dr
            lanes = slice(dr * 128, dr * 128 + 128)
            for at, col in ((0, 1), (64, 2), (512, 3), (576, 0)):
                where = base + at + k * 128
                if 0 <= a <= 2:
                    val = blocks[a][rows, col * 128 : col * 128 + 128]
                else:
                    val = jnp.zeros((64, 128), BF)
                w_ref[where : where + 64, lanes] = val


def prepare_enc(wenc, we):
    fill_full_res(we, 0, column_pairs(wenc, C0), slice(0, 64))


def prepare_down(wdown, wd):
    taps = nt(eye(C0), wdown[...].reshape(9 * C1, C0)).astype(BF)
    for k in range(4):
        for dr in range(2):
            a = k - dr
            for at, b in ((0, 0), (64, 2), (128, 1), (192, None)):
                where = k * 256 + at
                if b is not None and 0 <= a <= 2:
                    t = 3 * a + b
                    val = taps[:, t * 128 : t * 128 + 128]
                else:
                    val = jnp.zeros((64, 128), BF)
                wd[where : where + 64, dr * 128 : dr * 128 + 128] = val


def prepare_mid(wmid, wm):
    taps = nt(eye(C1), wmid[...].reshape(9 * C1, C1)).astype(BF)
    for k in range(4):
        for dr in range(2):
            a = k - dr
            for b in range(3):
                where = k * 384 + b * 128
                if 0 <= a <= 2:
                    t = 3 * a + b
                    val = taps[:, t * 128 : t * 128 + 128]
                else:
                    val = jnp.zeros((128, 128), BF)
                wm[where : where + 128, dr * 128 : dr * 128 + 128] = val


def prepare_unite(wun, wu):
    blocks = column_pairs(wun, 2 * C0)
    fill_full_res(wu, 0, blocks, slice(64, 128))
    fill_full_res(wu, 1024, blocks, slice(0, 64))


def stem_rows(x_ref, index, win_ref, fx, dest):
    fx[...] = x_ref[index].astype(F32).reshape(VARS * H, W)
    i, j = grid_iota(128, 128)
    spread = one_hot(j == 2 * (i % 64) + i // 64)
    win = win_ref[...]
    hi = upper_lanes(WP)

    def body(g, carry):
        rows = [fx[pl.ds(4 * g + k, VARS, stride=H), :].astype(BF) for k in range(4)]
        y = gelu(nn(win, jnp.concatenate(rows, axis=1))).astype(BF)
        stacked = jnp.concatenate([y[:, k * W : k * W + W] for k in range(4)], axis=0)
        z = nt(spread, stacked)
        for k in range(2):
            even = z[:WP, k * 128 : k * 128 + 128]
            odd = z[WP:, k * 128 : k * 128 + 128]
            dest[4 * g + 2 * k] = jnp.where(hi, pltpu.roll(odd, 64, 1), even).astype(BF)
            dest[4 * g + 2 * k + 1] = jnp.where(hi, odd, pltpu.roll(even, 64, 1)).astype(BF)
        return carry

    lax.fori_loop(0, H // 4, body, 0)


def edge_columns(main, low, high):
    def body(q, carry):
        r0, r1 = main.at[2 * q], main.at[2 * q + 1]
        low[q] = jnp.concatenate(
            [r0[0:16].astype(F32)[0:8], r1[0:16].astype(F32)[0:8]], axis=0
        ).astype(BF)
        high[q] = jnp.concatenate(
            [r0[48:64].astype(F32)[8:16], r1[48:64].astype(F32)[8:16]], axis=0
        ).astype(BF)
        return carry

    lax.fori_loop(0, HP, body, 0)


def widened(main, halo, f, ee, eb):
    top, bot, left, right, ctl, ctr, cbl, cbr = halo

    def sides(q, at, lref, rref):
        lv, rv = lref[q].astype(F32), rref[q].astype(F32)
        f[at, 8:16] = lv[0:8]
        f[at + 1, 8:16] = lv[8:16]
        f[at, 80:88] = rv[0:8]
        f[at + 1, 80:88] = rv[8:16]

    def own(q, carry):
        sides(q, 8 + 2 * q, left, right)
        f[8 + 2 * q, OWN] = main[2 * q].astype(F32)
        f[9 + 2 * q, OWN] = main[2 * q + 1].astype(F32)
        return carry

    def corner(q, carry):
        sides(q, 2 * q, ctl, ctr)
        sides(q, 24 + 2 * q, cbl, cbr)
        return carry

    def rims(t, carry):
        f[1 + t, OWN] = top[t].astype(F32)
        f[24 + t, OWN] = bot[t].astype(F32)
        return carry

    lax.fori_loop(0, HP, own, 0)
    lax.fori_loop(0, 4, corner, 0)
    lax.fori_loop(0, 7, rims, 0)
    hi = upper_lanes(EXT)

    def split(q, carry):
        for par in range(2):
            rr = 2 * q + par
            ee[par, q] = f[rr, MID].astype(BF)
            eb[par, q] = pltpu.roll(jnp.where(hi, f[rr, PREV], f[rr, NEXT]), 64, 1).astype(BF)
        return carry

    lax.fori_loop(0, 16, split, 0)


def quads(refs, first, count):
    pieces = []
    for ref in refs:
        for par, lag in ((1, 0), (0, 1), (1, 1), (0, 2)):
            v = ref[par, pl.ds(first + lag, count)]
            pieces.append(v.reshape(-1, v.shape[-1]))
    return jnp.concatenate(pieces, axis=1)


def kept(value, keep):
    return jnp.where(keep, value, 0.0)


def encoder(above, below, ee, eb, we, fs, fp, qc, qs, group):
    def body(g, carry):
        first = g * group
        y = rounded(gelu(nn(quads((ee, eb), first, group), we[...])))
        for p in range(group):
            ii = first + p
            keep = ((ii >= 3) | above) & ((ii <= 10) | below)
            v = kept(y[p * EXT : p * EXT + EXT], keep)
            v0, v1 = v[:, :128], v[:, 128:]
            fs[2 * ii, MID] = v0
            fs[2 * ii + 1, MID] = v1
            s = v0 + v1
            fp[ii, MID] = rounded((s + pltpu.roll(s, 64, 1)) * 0.25)
        return carry

    lax.fori_loop(0, 14 // group, body, 0)
    hi = upper_lanes(EXT)

    def split(q, carry):
        for par in range(2):
            ii = 2 * q + par
            qc[par, q] = fp[ii, MID].astype(BF)
            qs[par, q] = jnp.where(hi, fp[ii, NEXT], fp[ii, PREV]).astype(BF)
        return carry

    lax.fori_loop(0, 7, split, 0)


def row_quads(refs, first, count):
    pieces = []
    for lag in range(2):
        for par in range(2):
            for ref in refs:
                v = ref[par, pl.ds(first + lag, count)]
                pieces.append(v.reshape(-1, v.shape[-1]))
    return jnp.concatenate(pieces, axis=1)


def deepest(above, below, qc, qs, wd, wm, wup_ref, fd, dm, dc, dp, fl, group_d, group_m):
    def down(g, carry):
        first = g * group_d
        y = rounded(gelu(nn(row_quads((qs, qc), first, group_d), wd[...])))
        for p in range(group_d):
            k = first + p
            keep = ((k >= 1) | above) & ((k <= 4) | below)
            v = kept(y[p * EXT : p * EXT + EXT], keep)
            fd[2 * k, MID] = v[:, :128]
            fd[2 * k + 1, MID] = v[:, 128:]
        return carry

    lax.fori_loop(0, 6 // group_d, down, 0)

    def split(q, carry):
        for par in range(2):
            dd = 2 * q + par
            dm[par, q] = fd[dd, PREV].astype(BF)
            dc[par, q] = fd[dd, MID].astype(BF)
            dp[par, q] = fd[dd, NEXT].astype(BF)
        return carry

    lax.fori_loop(0, 6, split, 0)
    up = jnp.concatenate([wup_ref[...], wup_ref[...]], axis=0)

    def mid(g, carry):
        first = g * group_m
        y = gelu(nn(row_quads((dm, dc, dp), first, group_m), wm[...]))
        rows = []
        for p in range(group_m):
            k = first + p
            for dr in range(2):
                v = y[p * EXT : p * EXT + EXT, dr * 128 : dr * 128 + 128]
                v = v + fd[2 * k + 1 + dr, MID]
                if dr == 0:
                    keep = (k >= 1) | above
                else:
                    keep = (k <= 3) | below
                rows.append(kept(v, keep).astype(BF))
        z = rounded(nt(jnp.concatenate(rows, axis=0), up))
        for p in range(group_m):
            k = first + p
            for dr in range(2):
                at = (2 * p + dr) * EXT
                fl[2 * k + dr, MID] = z[at : at + EXT]
        return carry

    lax.fori_loop(0, 5 // group_m, mid, 0)


def join_operands(fs, fl, sc, sb, lc, lb):
    hi = upper_lanes(WP)

    def skip(q, carry):
        for par in range(2):
            idx = 2 * (q + 2) + par
            sc[par, q] = fs[idx, OWN].astype(BF)
            sb[par, q] = pltpu.roll(
                jnp.where(hi, fs[idx, OWN_PREV], fs[idx, OWN_NEXT]), 64, 1
            ).astype(BF)
        return carry

    lax.fori_loop(0, 10, skip, 0)

    def lift(m, carry):
        lc[m] = fl[m, OWN].astype(BF)
        lb[m] = jnp.where(hi, fl[m, OWN_NEXT], fl[m, OWN_PREV]).astype(BF)
        return carry

    lax.fori_loop(0, 10, lift, 0)


def unite(sc, sb, lc, lb, wu, first, group):
    pieces = [quads((sc, sb), first, group)]
    for ref in (lc, lb):
        for lag in (0, 1, 1, 2):
            pieces.append(ref[pl.ds(first + lag, group)].reshape(-1, 128))
    return gelu(nn(jnp.concatenate(pieces, axis=1), wu[...])).astype(BF)


def kernel(
    plan, x_ref, win, wenc, wdown, wmid, wup, wun, out_ref,
    fx, send_a, main_b, recv_a, low, high, top, bot, left, right, ctl, ctr, cbl, cbr,
    f, ee, eb, fs, fp, qc, qs, fd, dm, dc, dp, fl, sc, sb, lc, lb,
    merged_b, recv_b, we, wd, wm, wu,
    halo_send, halo_recv, a_send, a_recv, b_send, b_recv,
):
    section, lat, lon = lax.axis_index("section"), lax.axis_index("lat"), lax.axis_index("lon")
    lats, lons = lax.axis_size("lat"), lax.axis_size("lon")
    above, below = lat > 0, lat < lats - 1
    up, dn = jnp.maximum(lat - 1, 0), jnp.minimum(lat + 1, lats - 1)
    lt, rt = lax.rem(lon + lons - 1, lons), lax.rem(lon + 1, lons)
    partner = (1 - section, lat, lon)

    barrier = pltpu.get_barrier_semaphore()

    def greet(device):
        pl.semaphore_signal(barrier, inc=1, device_id=device, device_id_type=MESH)

    greet(partner)
    greet((section, lat, lt))
    greet((section, lat, rt))

    @pl.when(above)
    def _():
        for c in (lt, lon, rt):
            greet((section, up, c))

    @pl.when(below)
    def _():
        for c in (lt, lon, rt):
            greet((section, dn, c))

    index_a = lax.rem(jnp.where(section == 1, plan[0], plan[3]), 2)
    stem_rows(x_ref, index_a, win, fx, send_a)

    pl.semaphore_wait(barrier, 3 + jnp.where(above, 3, 0) + jnp.where(below, 3, 0))

    copy_a = pltpu.make_async_remote_copy(
        src_ref=send_a, dst_ref=recv_a, send_sem=a_send, recv_sem=a_recv,
        device_id=partner, device_id_type=MESH,
    )
    copy_a.start()

    def halo_copies(n, main):
        def rc(d, src, dst, device):
            return pltpu.make_async_remote_copy(
                src_ref=src, dst_ref=dst, send_sem=halo_send.at[n, d], recv_sem=halo_recv.at[n, d],
                device_id=device, device_id_type=MESH,
            )

        lo, hi = low.at[n], high.at[n]
        upward = [
            rc(0, main.at[0:7], bot.at[n], (section, up, lon)),
            rc(1, lo.at[0:4], cbr.at[n], (section, up, lt)),
            rc(2, hi.at[0:4], cbl.at[n], (section, up, rt)),
        ]
        downward = [
            rc(3, main.at[9:16], top.at[n], (section, dn, lon)),
            rc(4, lo.at[4:8], ctr.at[n], (section, dn, lt)),
            rc(5, hi.at[4:8], ctl.at[n], (section, dn, rt)),
        ]
        across = [
            rc(6, lo, right.at[n], (section, lat, lt)),
            rc(7, hi, left.at[n], (section, lat, rt)),
        ]
        return upward, downward, across

    def start_halo(n, main):
        edge_columns(main, low.at[n], high.at[n])
        upward, downward, across = halo_copies(n, main)

        @pl.when(above)
        def _():
            for c in upward:
                c.start()

        @pl.when(below)
        def _():
            for c in downward:
                c.start()

        for c in across:
            c.start()

        @pl.when(jnp.logical_not(above))
        def _():
            for ref in (top, ctl, ctr):
                ref[n] = jnp.zeros(ref.shape[1:], BF)

        @pl.when(jnp.logical_not(below))
        def _():
            for ref in (bot, cbl, cbr):
                ref[n] = jnp.zeros(ref.shape[1:], BF)

    def finish_halo(n, main):
        upward, downward, across = halo_copies(n, main)

        @pl.when(above)
        def _():
            for c in upward:
                c.wait_send()
            for c in downward:
                c.wait_recv()

        @pl.when(below)
        def _():
            for c in downward:
                c.wait_send()
            for c in upward:
                c.wait_recv()

        for c in across:
            c.wait()

    def halo(n):
        return [r.at[n] for r in (top, bot, left, right, ctl, ctr, cbl, cbr)]

    stem_rows(x_ref, 1 - index_a, win, fx, main_b)
    start_halo(0, main_b)

    prepare_enc(wenc, we)
    prepare_down(wdown, wd)
    prepare_mid(wmid, wm)
    prepare_unite(wun, wu)
    for ref in (f, fs, fp, fd, fl):
        rows = ref.shape[0]
        ref[:, 0:8] = jnp.zeros((rows, 8, 128), F32)
        ref[:, PADDED - 8 :] = jnp.zeros((rows, 8, 128), F32)

    finish_halo(0, main_b)
    widened(main_b, halo(0), f, ee, eb)
    encoder(above, below, ee, eb, we, fs, fp, qc, qs, 2)
    deepest(above, below, qc, qs, wd, wm, wup, fd, dm, dc, dp, fl, 2, 1)

    copy_a.wait()
    start_halo(1, recv_a)

    join_operands(fs, fl, sc, sb, lc, lb)

    def copy_b(g):
        rows = pl.ds(g * 2, 2)
        return pltpu.make_async_remote_copy(
            src_ref=merged_b.at[rows], dst_ref=recv_b.at[rows],
            send_sem=b_send.at[g], recv_sem=b_recv.at[g],
            device_id=partner, device_id_type=MESH,
        )

    def unite_b(g, carry):
        merged_b[pl.ds(2 * g, 2)] = unite(sc, sb, lc, lb, wu, 2 * g, 2).reshape(2, WP, 256)
        copy_b(g).start()
        return carry

    lax.fori_loop(0, 4, unite_b, 0)

    finish_halo(1, recv_a)
    widened(recv_a, halo(1), f, ee, eb)
    encoder(above, below, ee, eb, we, fs, fp, qc, qs, 2)
    deepest(above, below, qc, qs, wd, wm, wup, fd, dm, dc, dp, fl, 2, 1)
    join_operands(fs, fl, sc, sb, lc, lb)

    def unite_a(g, carry):
        out_ref[section, pl.ds(2 * g, 2)] = unite(sc, sb, lc, lb, wu, 2 * g, 2).reshape(2, WP, 256)
        return carry

    lax.fori_loop(0, 4, unite_a, 0)

    for g in range(4):
        copy_b(g).wait()
    stays = jnp.where(section == 0, plan[1] < 2, plan[2] >= 2)

    def choose(i, carry):
        out_ref[1 - section, i] = jnp.where(stays, merged_b[i], recv_b[i])
        return carry

    lax.fori_loop(0, HP, choose, 0)


def project(m_ref, wout_ref, out_ref, fo):
    w = wout_ref[...]
    zero = jnp.zeros((VARS, C0), BF)
    both = jnp.concatenate(
        [jnp.concatenate([w, zero], axis=1), jnp.concatenate([zero, w], axis=1)], axis=0
    )
    i, j = grid_iota(256, 256)
    gather = one_hot((i // 64 % 2 == j // 128) & (j % 128 == 2 * (i % 64) + i // 128))
    for p in range(HP):
        m = m_ref[0, p]
        rows = jnp.concatenate([m[:, :128], m[:, 128:]], axis=0)
        u = nt(both, rows).astype(BF)
        v = nn(jnp.concatenate([u[:VARS], u[VARS:]], axis=1), gather)
        fo[pl.ds(2 * p, VARS, stride=H), :] = v[:, :128]
        fo[pl.ds(2 * p + 1, VARS, stride=H), :] = v[:, 128:]
    out_ref[0] = fo[...].reshape(VARS, H, W).astype(BF)


def shards(fields_in, plan, in_proj, enc_conv, down_conv, mid_conv, up_proj, unite_conv, out_proj):
    vmem = pl.BlockSpec(memory_space=pltpu.VMEM)
    dma = pltpu.SemaphoreType.DMA
    bf = lambda *s: pltpu.VMEM(s, BF)
    fl = lambda *s: pltpu.VMEM(s, F32)
    merged = pl.pallas_call(
        kernel,
        name="unet",
        out_shape=jax.ShapeDtypeStruct((2, HP, WP, 256), BF),
        in_specs=[pl.BlockSpec(memory_space=pltpu.SMEM)] + [vmem] * 7,
        out_specs=vmem,
        scratch_shapes=[
            fl(VARS * H, W),
            bf(H, WP, 128), bf(H, WP, 128), bf(H, WP, 128),
            bf(2, 8, 16, 128), bf(2, 8, 16, 128),
            bf(2, 7, WP, 128), bf(2, 7, WP, 128),
            bf(2, 8, 16, 128), bf(2, 8, 16, 128),
            bf(2, 4, 16, 128), bf(2, 4, 16, 128), bf(2, 4, 16, 128), bf(2, 4, 16, 128),
            fl(32, PADDED, 128), bf(2, 16, EXT, 128), bf(2, 16, EXT, 128),
            fl(28, PADDED, 128), fl(14, PADDED, 128), bf(2, 7, EXT, 128), bf(2, 7, EXT, 128),
            fl(12, PADDED, 128), bf(2, 6, EXT, 128), bf(2, 6, EXT, 128), bf(2, 6, EXT, 128),
            fl(10, PADDED, 128),
            bf(2, 10, WP, 128), bf(2, 10, WP, 128), bf(10, WP, 128), bf(10, WP, 128),
            bf(HP, WP, 256), bf(HP, WP, 256),
            bf(1024, 256), bf(1024, 256), bf(1536, 256), bf(2048, 256),
            dma((2, 8)), dma((2, 8)), dma, dma, dma((4,)), dma((4,)),
        ],
        compiler_params=pltpu.CompilerParams(
            collective_id=0, has_side_effects=True, vmem_limit_bytes=40 * 2**20
        ),
    )(plan, fields_in, in_proj, enc_conv, down_conv, mid_conv, up_proj, unite_conv)
    return pl.pallas_call(
        project,
        name="project",
        grid=(2,),
        out_shape=jax.ShapeDtypeStruct((2, VARS, H, W), BF),
        in_specs=[
            pl.BlockSpec((1, HP, WP, 256), lambda t: (t, 0, 0, 0)),
            pl.BlockSpec((VARS, C0), lambda t: (0, 0)),
        ],
        out_specs=pl.BlockSpec((1, VARS, H, W), lambda t: (t, 0, 0, 0)),
        scratch_shapes=[pltpu.VMEM((VARS * H, W), F32)],
    )(merged, out_proj)


def solution(mesh):
    return jax.shard_map(
        shards,
        mesh=mesh,
        in_specs=(P("section", None, "lat", "lon"), P(), P(), P(), P(), P(), P(), P(), P()),
        out_specs=P("section", None, "lat", "lon"),
        check_vma=False,
    )
```

time: 123 us -> 53 us (0.43)
  the two profiles are of different devices: /device:TPU:56 before, /device:TPU:6 now
where the time goes in v1:
time: 53 us; the launch traced here: 52.8 us
  Pallas kernels  47.2 us (89%)
  local copies, waits for them, and re-layouts  5.45 us (10%)
    pallas_call x1, Pallas kernels, shards(): pl.pallas_call(kernel, name='unet', out_shape=jax.ShapeDtypeStruct((2, HP...  44.2 us
    unnamed x18, local copies, waits for them, and re-layouts  5.45 us
    pallas_call x1, Pallas kernels, shards(): pl.pallas_call(project, name='project', grid=(2,), out_shape=jax.ShapeDty...  3.05 us

profile of v1, /device:TPU:6, one launch (start us, length us, event | category | flops | bytes accessed | tf_op | source)
XLA Modules:
  0.0 52.8 jit_solution(16193835168502094308)
XLA Ops:
  0.0 0.0 copy-start.2
  0.0 1.5 %copy.11.wout_ref = bf16[96,64]{1,0:T(8,128)(2,1)} copy(bf16[96,64]{0,1:T(8,128)(2,1)} %param.17) | data formatting | bytes 24576 | tf_op args[8]
  1.5 0.0 copy-start.3
  1.5 0.0 copy-start.5
  1.5 0.0 copy-start.6
  1.5 0.0 copy-start.7
  1.5 1.2 %copy.10.wdown = bf16[9,128,64]{2,1,0:T(8,128)(2,1)S(1)} copy(bf16[9,128,64]{1,2,0:T(8,128)(2,1)} %param.13) | data formatting | bytes 294912 | tf_op args[4]
  2.6 0.0 copy-done.2
  2.6 0.0 copy-done.3
  2.6 0.0 copy-done.5
  2.7 0.0 copy-done.6
  2.7 0.0 copy-done.7
  2.7 0.0 copy-start.1
  2.7 1.1 %copy-done.1 = bf16[2,96,16,128]{3,2,1,0:T(8,128)(2,1)S(1)} copy-done((bf16[2,96,16,128]{3,2,1,0:T(8,128)(2,1)S(1)}, bf16[2,96,16,128]{3,2,1,0:T(8,128)(2,1)}, u32[]{:S(2)}) %copy-start.1) | copy-done | bytes 786456
  3.8 0.0 copy-start.4
  3.8 0.9 %copy-done.4 = bf16[9,64,128]{2,1,0:T(8,128)(2,1)S(1)} copy-done((bf16[9,64,128]{2,1,0:T(8,128)(2,1)S(1)}, bf16[9,64,128]{2,1,0:T(8,128)(2,1)}, u32[]{:S(2)}) %copy-start.4) | copy-done | bytes 147480
  4.7 44.2 %unet.1.m_ref = bf16[2,8,64,256]{3,2,1,0:T(8,128)(2,1)S(1)} custom-call(s32[4]{0:T(128)S(1)} %copy-done.7, bf16[2,96,16,128]{3,2,1,0:T(8,128)(2,1)S(1)} %copy-done.1, bf16[64,96]{1,0:T(8,128)(2,1)S(1)} %copy-done.5, bf16[9,64,64]{2,1,0:T(8,128)(2,1)S(1)} %copy-done.3, bf16[9,128,64]{2,1,0:T(8,128)(2,1)S(1)} %copy.10.wdown, ...), custom_call_target="tpu_custom_call" | custom-call | tf_op jit(solution)/shard_map/unet/pallas_call | solution.py:536
  48.9 0.0 copy-start
  48.9 0.8 %copy-done = bf16[2,8,64,256]{3,2,1,0:T(8,128)(2,1)} copy-done((bf16[2,8,64,256]{3,2,1,0:T(8,128)(2,1)}, bf16[2,8,64,256]{3,2,1,0:T(8,128)(2,1)S(1)}, u32[]{:S(2)}) %copy-start) | copy-done | bytes 524312
  49.7 3.1 %project.1 = bf16[2,96,16,128]{3,2,1,0:T(8,128)(2,1)} custom-call(bf16[2,8,64,256]{3,2,1,0:T(8,128)(2,1)} %copy-done, bf16[96,64]{1,0:T(8,128)(2,1)} %copy.11.wout_ref), custom_call_target="tpu_custom_call" | custom-call | tf_op jit(solution)/shard_map/project/pallas_call | solution.py:562
Async XLA Ops:
  0.0 2.6 %copy-start.2 = (bf16[9,128,128]{2,1,0:T(8,128)(2,1)S(1)}, bf16[9,128,128]{2,1,0:T(8,128)(2,1)}, u32[]{:S(2)}) copy-start(bf16[9,128,128]{2,1,0:T(8,128)(2,1)} %wmid.1) | copy-start | bytes 884740
  1.5 1.2 %copy-start.3 = (bf16[9,64,64]{2,1,0:T(8,128)(2,1)S(1)}, bf16[9,64,64]{2,1,0:T(8,128)(2,1)}, u32[]{:S(2)}) copy-start(bf16[9,64,64]{2,1,0:T(8,128)(2,1)} %wenc.1) | copy-start | bytes 221188
  1.5 1.2 %copy-start.5 = (bf16[64,96]{1,0:T(8,128)(2,1)S(1)}, bf16[64,96]{1,0:T(8,128)(2,1)}, u32[]{:S(2)}) copy-start(bf16[64,96]{1,0:T(8,128)(2,1)} %win.1) | copy-start | bytes 36868
  1.5 1.2 %copy-start.6 = (bf16[64,128]{1,0:T(8,128)(2,1)S(1)}, bf16[64,128]{1,0:T(8,128)(2,1)}, u32[]{:S(2)}) copy-start(bf16[64,128]{1,0:T(8,128)(2,1)} %wup.1) | copy-start | bytes 49156
  1.5 1.2 %copy-start.7 = (s32[4]{0:T(128)S(1)}, s32[4]{0:T(128)}, u32[]{:S(2)}) copy-start(s32[4]{0:T(128)} %plan.1) | copy-start | bytes 52
  2.7 1.1 %copy-start.1 = (bf16[2,96,16,128]{3,2,1,0:T(8,128)(2,1)S(1)}, bf16[2,96,16,128]{3,2,1,0:T(8,128)(2,1)}, u32[]{:S(2)}) copy-start(bf16[2,96,16,128]{3,2,1,0:T(8,128)(2,1)} %x_ref.1) | copy-start | bytes 2359300
  3.8 0.9 %copy-start.4 = (bf16[9,64,128]{2,1,0:T(8,128)(2,1)S(1)}, bf16[9,64,128]{2,1,0:T(8,128)(2,1)}, u32[]{:S(2)}) copy-start(bf16[9,64,128]{2,1,0:T(8,128)(2,1)} %wun.1) | copy-start | bytes 442372
  48.9 0.8 %copy-start = (bf16[2,8,64,256]{3,2,1,0:T(8,128)(2,1)}, bf16[2,8,64,256]{3,2,1,0:T(8,128)(2,1)S(1)}, u32[]{:S(2)}) copy-start(bf16[2,8,64,256]{3,2,1,0:T(8,128)(2,1)S(1)} %unet.1.m_ref) | copy-start | bytes 1572868

commit v2 on v1

v2 whole, which is shorter than its diff:
```python
import functools

import jax
import jax.numpy as jnp
from jax import lax
from jax.experimental import pallas as pl
from jax.experimental.pallas import tpu as pltpu
from jax.sharding import PartitionSpec as P

F32, BF = jnp.float32, jnp.bfloat16
MESH = pl.DeviceIdType.MESH

VARS, C0, C1 = 96, 64, 128
H, W = 16, 128
HP, WP = H // 2, W // 2
EXT = WP + 16
PADDED = EXT + 16
MID = slice(8, 8 + EXT)
PREV = slice(7, 7 + EXT)
NEXT = slice(9, 9 + EXT)
OWN = slice(16, 16 + WP)
OWN_PREV = slice(15, 15 + WP)
OWN_NEXT = slice(17, 17 + WP)


def gelu(x):
    half = 0.5 * x
    inner = x * (0.7978845608028654 + 0.035677408136300125 * (x * x))
    return half + half * jnp.tanh(inner)


def rounded(x):
    return x.astype(BF).astype(F32)


def nn(a, b):
    return jnp.dot(a, b, preferred_element_type=F32)


def nt(a, b):
    return lax.dot_general(a, b, (((1,), (1,)), ((), ())), preferred_element_type=F32)


def grid_iota(rows, cols):
    shape = (rows, cols)
    return lax.broadcasted_iota(jnp.int32, shape, 0), lax.broadcasted_iota(jnp.int32, shape, 1)


def one_hot(mask):
    return jnp.where(mask, 1.0, 0.0).astype(BF)


def loop(count, step, body):
    def several(i, carry):
        for k in range(step):
            body(i * step + k)
        return carry

    if count == step:
        several(0, 0)
    else:
        lax.fori_loop(0, count // step, several, 0)


def eye(n):
    i, j = grid_iota(n, n)
    return one_hot(i == j)


def upper_lanes(rows):
    return lax.broadcasted_iota(jnp.int32, (rows, 128), 1) >= 64


def column_pairs(taps, channels):
    zero = jnp.zeros((C0, channels), BF)
    unit = eye(channels)
    out = []
    for a in range(3):
        b0, b1, b2 = taps[3 * a], taps[3 * a + 1], taps[3 * a + 2]
        stacked = jnp.concatenate([zero, b2, b1, b0, b2, b1, b0, zero], axis=0)
        out.append(nt(unit, stacked).astype(BF))
    return out


def fill_full_res(w_ref, base, blocks, rows):
    for k in range(4):
        for dr in range(2):
            a = k - dr
            lanes = slice(dr * 128, dr * 128 + 128)
            for at, col in ((0, 1), (64, 2), (512, 3), (576, 0)):
                where = base + at + k * 128
                if 0 <= a <= 2:
                    val = blocks[a][rows, col * 128 : col * 128 + 128]
                else:
                    val = jnp.zeros((64, 128), BF)
                w_ref[where : where + 64, lanes] = val


def prepare_enc(wenc, we):
    fill_full_res(we, 0, column_pairs(wenc, C0), slice(0, 64))


def prepare_down(wdown, wd):
    for k in range(4):
        for dr in range(2):
            a = k - dr
            for at, b in ((0, 0), (64, 2), (128, 1), (192, None)):
                where = k * 256 + at
                if b is not None and 0 <= a <= 2:
                    val = wdown[3 * a + b]
                else:
                    val = jnp.zeros((64, 128), BF)
                wd[where : where + 64, dr * 128 : dr * 128 + 128] = val


def prepare_mid(wmid, wm):
    taps = nt(eye(C1), wmid[...].reshape(9 * C1, C1)).astype(BF)
    for k in range(4):
        for dr in range(2):
            a = k - dr
            for b in range(3):
                where = k * 384 + b * 128
                if 0 <= a <= 2:
                    t = 3 * a + b
                    val = taps[:, t * 128 : t * 128 + 128]
                else:
                    val = jnp.zeros((128, 128), BF)
                wm[where : where + 128, dr * 128 : dr * 128 + 128] = val


def prepare_unite(wun, wu):
    blocks = column_pairs(wun, 2 * C0)
    fill_full_res(wu, 0, blocks, slice(64, 128))
    fill_full_res(wu, 1024, blocks, slice(0, 64))


def stem_rows(x_ref, index, win_ref, fx, dest, half):
    if half == 0:
        fx[...] = x_ref[index].astype(F32).reshape(VARS * H, W)
    i, j = grid_iota(128, 128)
    spread = one_hot(j == 2 * (i % 64) + i // 64)
    win = win_ref[...]
    hi = upper_lanes(WP)

    def body(g):
        first = 8 * half + 4 * g
        rows = [fx[pl.ds(first + k, VARS, stride=H), :].astype(BF) for k in range(4)]
        y = gelu(nn(win, jnp.concatenate(rows, axis=1))).astype(BF)
        stacked = jnp.concatenate([y[:, k * W : k * W + W] for k in range(4)], axis=0)
        z = nt(spread, stacked)
        for k in range(2):
            even = z[:WP, k * 128 : k * 128 + 128]
            odd = z[WP:, k * 128 : k * 128 + 128]
            at = first + 2 * k
            dest[at] = jnp.where(hi, pltpu.roll(odd, 64, 1), even).astype(BF)
            dest[at + 1] = jnp.where(hi, odd, pltpu.roll(even, 64, 1)).astype(BF)

    loop(2, 2, body)


def edge_columns(main, low, high, half):
    def body(k):
        q = 4 * half + k
        r0, r1 = main.at[2 * q], main.at[2 * q + 1]
        low[q] = jnp.concatenate(
            [r0[0:16].astype(F32)[0:8], r1[0:16].astype(F32)[0:8]], axis=0
        ).astype(BF)
        high[q] = jnp.concatenate(
            [r0[48:64].astype(F32)[8:16], r1[48:64].astype(F32)[8:16]], axis=0
        ).astype(BF)

    loop(4, 4, body)


def widened(main, halo, f, ee, eb):
    top, bot, left, right, ctl, ctr, cbl, cbr = halo

    def sides(q, at, lref, rref):
        lv, rv = lref[q].astype(F32), rref[q].astype(F32)
        f[at, 8:16] = lv[0:8]
        f[at + 1, 8:16] = lv[8:16]
        f[at, 80:88] = rv[0:8]
        f[at + 1, 80:88] = rv[8:16]

    def own(q):
        sides(q, 8 + 2 * q, left, right)
        f[8 + 2 * q, OWN] = main[2 * q].astype(F32)
        f[9 + 2 * q, OWN] = main[2 * q + 1].astype(F32)

    def corner(q):
        sides(q, 2 * q, ctl, ctr)
        sides(q, 24 + 2 * q, cbl, cbr)

    def rims(t):
        f[1 + t, OWN] = top[t].astype(F32)
        f[24 + t, OWN] = bot[t].astype(F32)

    loop(HP, 4, own)
    loop(4, 4, corner)
    loop(7, 7, rims)
    hi = upper_lanes(EXT)

    def split(q):
        for par in range(2):
            rr = 2 * q + par
            ee[par, q] = f[rr, MID].astype(BF)
            eb[par, q] = pltpu.roll(jnp.where(hi, f[rr, PREV], f[rr, NEXT]), 64, 1).astype(BF)

    loop(16, 4, split)


def quads(refs, first, count):
    pieces = []
    for ref in refs:
        for par, lag in ((1, 0), (0, 1), (1, 1), (0, 2)):
            v = ref[par, pl.ds(first + lag, count)]
            pieces.append(v.reshape(-1, v.shape[-1]))
    return jnp.concatenate(pieces, axis=1)


def kept(value, keep):
    return jnp.where(keep, value, 0.0)


def encoder(above, below, ee, eb, we, fs, fp, qc, qs, group):
    def body(g):
        first = g * group
        y = rounded(gelu(nn(quads((ee, eb), first, group), we[...])))
        for p in range(group):
            ii = first + p
            keep = ((ii >= 3) | above) & ((ii <= 10) | below)
            v = kept(y[p * EXT : p * EXT + EXT], keep)
            v0, v1 = v[:, :128], v[:, 128:]
            fs[2 * ii, MID] = v0
            fs[2 * ii + 1, MID] = v1
            s = v0 + v1
            fp[ii, MID] = rounded((s + pltpu.roll(s, 64, 1)) * 0.25)

    loop(14 // group, 1, body)
    hi = upper_lanes(EXT)

    def split(q):
        for par in range(2):
            ii = 2 * q + par
            qc[par, q] = fp[ii, MID].astype(BF)
            qs[par, q] = jnp.where(hi, fp[ii, NEXT], fp[ii, PREV]).astype(BF)

    loop(7, 7, split)


def row_quads(refs, first, count):
    pieces = []
    for lag in range(2):
        for par in range(2):
            for ref in refs:
                v = ref[par, pl.ds(first + lag, count)]
                pieces.append(v.reshape(-1, v.shape[-1]))
    return jnp.concatenate(pieces, axis=1)


def deepen(above, below, qc, qs, wd, fd, dm, dc, dp, group_d):
    def down(g):
        first = g * group_d
        y = rounded(gelu(nn(row_quads((qs, qc), first, group_d), wd[...])))
        for p in range(group_d):
            k = first + p
            keep = ((k >= 1) | above) & ((k <= 4) | below)
            v = kept(y[p * EXT : p * EXT + EXT], keep)
            fd[2 * k, MID] = v[:, :128]
            fd[2 * k + 1, MID] = v[:, 128:]

    loop(6 // group_d, 1, down)

    def split(q):
        for par in range(2):
            dd = 2 * q + par
            dm[par, q] = fd[dd, PREV].astype(BF)
            dc[par, q] = fd[dd, MID].astype(BF)
            dp[par, q] = fd[dd, NEXT].astype(BF)

    loop(6, 3, split)


def lift(above, below, dm, dc, dp, fd, wm, wup_ref, fl, group_m):
    up = jnp.concatenate([wup_ref[...], wup_ref[...]], axis=0)

    def mid(g):
        first = g * group_m
        y = gelu(nn(row_quads((dm, dc, dp), first, group_m), wm[...]))
        rows = []
        for p in range(group_m):
            k = first + p
            for dr in range(2):
                v = y[p * EXT : p * EXT + EXT, dr * 128 : dr * 128 + 128]
                v = v + fd[2 * k + 1 + dr, MID]
                if dr == 0:
                    keep = (k >= 1) | above
                else:
                    keep = (k <= 3) | below
                rows.append(kept(v, keep).astype(BF))
        z = rounded(nt(jnp.concatenate(rows, axis=0), up))
        for p in range(group_m):
            k = first + p
            for dr in range(2):
                at = (2 * p + dr) * EXT
                fl[2 * k + dr, MID] = z[at : at + EXT]

    loop(5 // group_m, 1, mid)


def join_operands(fs, fl, sc, sb, lc, lb):
    hi = upper_lanes(WP)

    def skip(q):
        for par in range(2):
            idx = 2 * (q + 2) + par
            sc[par, q] = fs[idx, OWN].astype(BF)
            sb[par, q] = pltpu.roll(
                jnp.where(hi, fs[idx, OWN_PREV], fs[idx, OWN_NEXT]), 64, 1
            ).astype(BF)

    loop(10, 5, skip)

    def lift(m):
        lc[m] = fl[m, OWN].astype(BF)
        lb[m] = jnp.where(hi, fl[m, OWN_NEXT], fl[m, OWN_PREV]).astype(BF)

    loop(10, 10, lift)


def unite(sc, sb, lc, lb, wu, first, group):
    pieces = [quads((sc, sb), first, group)]
    for ref in (lc, lb):
        for lag in (0, 1, 1, 2):
            pieces.append(ref[pl.ds(first + lag, group)].reshape(-1, 128))
    return gelu(nn(jnp.concatenate(pieces, axis=1), wu[...])).astype(BF)


def kernel(
    plan, x_hbm, win_hbm, wenc_hbm, wdown_hbm, wmid_hbm, wup_hbm, wun_hbm, out_hbm,
    x_ref, win, wenc, wdown, wmid, wup, wun,
    fx, send_a, main_b, recv_a, low, high, top, bot, left, right, ctl, ctr, cbl, cbr,
    f, ee, eb, fs, fp, qc, qs, fd, dm, dc, dp, fl, sc, sb, lc, lb,
    merged_a, merged_b, recv_b, we, wd, wm, wu,
    x_sem, w_sem, out_sem, halo_send, halo_recv, a_send, a_recv, b_send, b_recv,
):
    section, lat, lon = lax.axis_index("section"), lax.axis_index("lat"), lax.axis_index("lon")
    lats, lons = lax.axis_size("lat"), lax.axis_size("lon")
    above, below = lat > 0, lat < lats - 1
    up, dn = jnp.maximum(lat - 1, 0), jnp.minimum(lat + 1, lats - 1)
    lt, rt = lax.rem(lon + lons - 1, lons), lax.rem(lon + 1, lons)
    partner = (1 - section, lat, lon)

    loads_w = [
        pltpu.make_async_copy(src, dst, w_sem.at[n])
        for n, (src, dst) in enumerate(
            (
                (win_hbm, win),
                (wenc_hbm, wenc),
                (wdown_hbm, wdown),
                (wmid_hbm, wmid),
                (wup_hbm, wup),
                (wun_hbm, wun),
            )
        )
    ]
    loads_x = [
        pltpu.make_async_copy(
            x_hbm.at[n // 4, pl.ds(n % 4 * 24, 24)],
            x_ref.at[n // 4, pl.ds(n % 4 * 24, 24)],
            x_sem.at[n],
        )
        for n in range(8)
    ]
    loads_w[0].start()
    for c in loads_x:
        c.start()
    for c in loads_w[1:]:
        c.start()

    barrier = pltpu.get_barrier_semaphore()

    def greet(device):
        pl.semaphore_signal(barrier, inc=1, device_id=device, device_id_type=MESH)

    greet(partner)
    greet((section, lat, lt))
    greet((section, lat, rt))

    @pl.when(above)
    def _():
        for c in (lt, lon, rt):
            greet((section, up, c))

    @pl.when(below)
    def _():
        for c in (lt, lon, rt):
            greet((section, dn, c))

    def copy_a(half):
        rows = pl.ds(8 * half, 8)
        return pltpu.make_async_remote_copy(
            src_ref=send_a.at[rows], dst_ref=recv_a.at[rows],
            send_sem=a_send.at[half], recv_sem=a_recv.at[half],
            device_id=partner, device_id_type=MESH,
        )

    def copy_b(half):
        rows = pl.ds(4 * half, 4)
        return pltpu.make_async_remote_copy(
            src_ref=merged_b.at[rows], dst_ref=recv_b.at[rows],
            send_sem=b_send.at[half], recv_sem=b_recv.at[half],
            device_id=partner, device_id_type=MESH,
        )

    def halo_copies(n, main, half):
        def rc(d, src, dst, device):
            return pltpu.make_async_remote_copy(
                src_ref=src, dst_ref=dst,
                send_sem=halo_send.at[n, d + 5 * half], recv_sem=halo_recv.at[n, d + 5 * half],
                device_id=device, device_id_type=MESH,
            )

        part = pl.ds(4 * half, 4)
        lo, hi = low.at[n, part], high.at[n, part]
        if half == 0:
            lat_to, rim, rim_to, lo_to, hi_to = up, main.at[0:7], bot, cbr, cbl
        else:
            lat_to, rim, rim_to, lo_to, hi_to = dn, main.at[9:16], top, ctr, ctl
        beyond = [
            rc(0, rim, rim_to.at[n], (section, lat_to, lon)),
            rc(1, lo, lo_to.at[n], (section, lat_to, lt)),
            rc(2, hi, hi_to.at[n], (section, lat_to, rt)),
        ]
        across = [
            rc(3, lo, right.at[n, part], (section, lat, lt)),
            rc(4, hi, left.at[n, part], (section, lat, rt)),
        ]
        return beyond, across

    def start_halo(n, main, half):
        edge_columns(main, low.at[n], high.at[n], half)
        beyond, across = halo_copies(n, main, half)

        @pl.when(below if half else above)
        def _():
            for c in beyond:
                c.start()

        for c in across:
            c.start()

    def finish_halo(n, main):
        upward, across0 = halo_copies(n, main, 0)
        downward, across1 = halo_copies(n, main, 1)
        for c in across0 + across1:
            c.wait()

        @pl.when(above)
        def _():
            for c in upward:
                c.wait_send()
            for c in downward:
                c.wait_recv()

        @pl.when(below)
        def _():
            for c in downward:
                c.wait_send()
            for c in upward:
                c.wait_recv()

    def halo(n):
        return [r.at[n] for r in (top, bot, left, right, ctl, ctr, cbl, cbr)]

    greeted = 3 + jnp.where(above, 3, 0) + jnp.where(below, 3, 0)
    index_a = lax.rem(jnp.where(section == 1, plan[0], plan[3]), 2)
    loads_w[0].wait()
    for c in loads_x:
        c.wait()
    for half in range(2):
        stem_rows(x_ref, 1 - index_a, win, fx, main_b, half)
    pl.semaphore_wait(barrier, greeted)
    for half in range(2):
        start_halo(0, main_b, half)
    for half in range(2):
        stem_rows(x_ref, index_a, win, fx, send_a, half)
        copy_a(half).start()

    for n in range(2):

        @pl.when(jnp.logical_not(above))
        def _():
            for ref in (top, ctl, ctr):
                ref[n] = jnp.zeros(ref.shape[1:], BF)

        @pl.when(jnp.logical_not(below))
        def _():
            for ref in (bot, cbl, cbr):
                ref[n] = jnp.zeros(ref.shape[1:], BF)

    for ref in (f, fs, fp, fd, fl):
        rows = ref.shape[0]
        ref[:, 0:8] = jnp.zeros((rows, 8, 128), F32)
        ref[:, PADDED - 8 :] = jnp.zeros((rows, 8, 128), F32)
    for c in loads_w[1:]:
        c.wait()
    prepare_enc(wenc, we)
    prepare_down(wdown, wd)
    prepare_mid(wmid, wm)
    prepare_unite(wun, wu)

    finish_halo(0, main_b)
    widened(main_b, halo(0), f, ee, eb)
    copy_a(0).wait()
    start_halo(1, recv_a, 0)
    encoder(above, below, ee, eb, we, fs, fp, qc, qs, 14)
    deepen(above, below, qc, qs, wd, fd, dm, dc, dp, 3)
    copy_a(1).wait()
    start_halo(1, recv_a, 1)
    lift(above, below, dm, dc, dp, fd, wm, wup, fl, 5)
    join_operands(fs, fl, sc, sb, lc, lb)

    for half in range(2):
        merged_b[pl.ds(4 * half, 4)] = unite(sc, sb, lc, lb, wu, 4 * half, 4).reshape(4, WP, 256)
        copy_b(half).start()

    finish_halo(1, recv_a)
    widened(recv_a, halo(1), f, ee, eb)
    encoder(above, below, ee, eb, we, fs, fp, qc, qs, 14)
    deepen(above, below, qc, qs, wd, fd, dm, dc, dp, 3)
    lift(above, below, dm, dc, dp, fd, wm, wup, fl, 5)
    join_operands(fs, fl, sc, sb, lc, lb)
    merged_a[...] = unite(sc, sb, lc, lb, wu, 0, 8).reshape(8, WP, 256)
    store_a = pltpu.make_async_copy(merged_a, out_hbm.at[section], out_sem.at[0])
    store_a.start()

    for half in range(2):
        copy_b(half).wait()
    stays = jnp.where(section == 0, plan[1] < 2, plan[2] >= 2)

    def choose(i):
        merged_b[i] = jnp.where(stays, merged_b[i], recv_b[i])

    loop(HP, 4, choose)
    store_b = pltpu.make_async_copy(merged_b, out_hbm.at[1 - section], out_sem.at[1])
    store_b.start()
    store_a.wait()
    store_b.wait()


def project(m_hbm, wout_ref, out_hbm, m_ref, fo, buf, load_sems, sems):
    loads = [pltpu.make_async_copy(m_hbm.at[t], m_ref.at[t], load_sems.at[t]) for t in range(2)]
    for load in loads:
        load.start()
    w = nt(eye(VARS), wout_ref[...]).astype(BF)
    zero = jnp.zeros((VARS, C0), BF)
    both = jnp.concatenate(
        [jnp.concatenate([w, zero], axis=1), jnp.concatenate([zero, w], axis=1)], axis=0
    )
    i, j = grid_iota(256, 256)
    gather = one_hot((i // 64 % 2 == j // 128) & (j % 128 == 2 * (i % 64) + i // 128))
    copies = []
    for t in range(2):
        loads[t].wait()
        parts = []
        for p in range(0, HP, 2):
            m = [m_ref[t, p + k // 2][:, k % 2 * 128 : k % 2 * 128 + 128] for k in range(4)]
            u = nt(both, jnp.concatenate(m, axis=0)).astype(BF)
            for k in range(2):
                lanes = slice(k * 128, k * 128 + 128)
                parts.append(jnp.concatenate([u[:VARS, lanes], u[VARS:, lanes]], axis=1))
        v = nn(jnp.concatenate(parts, axis=0), gather)
        for h in range(H):
            rows = v[h // 2 * VARS : h // 2 * VARS + VARS]
            fo[t, pl.ds(h, VARS, stride=H), :] = rows[:, h % 2 * 128 : h % 2 * 128 + 128]
        buf[t] = fo[t].reshape(VARS, H, W).astype(BF)
        copy = pltpu.make_async_copy(buf.at[t], out_hbm.at[t], sems.at[t])
        copy.start()
        copies.append(copy)
    for copy in copies:
        copy.wait()


def shards(fields_in, plan, in_proj, enc_conv, down_conv, mid_conv, up_proj, unite_conv, out_proj):
    vmem = pl.BlockSpec(memory_space=pltpu.VMEM)
    hbm = pl.BlockSpec(memory_space=pltpu.HBM)
    dma = pltpu.SemaphoreType.DMA
    bf = lambda *s: pltpu.VMEM(s, BF)
    fl = lambda *s: pltpu.VMEM(s, F32)
    merged = pl.pallas_call(
        kernel,
        name="unet",
        out_shape=jax.ShapeDtypeStruct((2, HP, WP, 256), BF),
        in_specs=[pl.BlockSpec(memory_space=pltpu.SMEM)] + [hbm] * 7,
        out_specs=hbm,
        scratch_shapes=[
            bf(2, VARS, H, W), bf(C0, VARS), bf(9, C0, C0), bf(9, C0, C1), bf(9, C1, C1),
            bf(C0, C1), bf(9, C0, C1),
            fl(VARS * H, W),
            bf(H, WP, 128), bf(H, WP, 128), bf(H, WP, 128),
            bf(2, 8, 16, 128), bf(2, 8, 16, 128),
            bf(2, 7, WP, 128), bf(2, 7, WP, 128),
            bf(2, 8, 16, 128), bf(2, 8, 16, 128),
            bf(2, 4, 16, 128), bf(2, 4, 16, 128), bf(2, 4, 16, 128), bf(2, 4, 16, 128),
            fl(32, PADDED, 128), bf(2, 16, EXT, 128), bf(2, 16, EXT, 128),
            fl(28, PADDED, 128), fl(14, PADDED, 128), bf(2, 7, EXT, 128), bf(2, 7, EXT, 128),
            fl(12, PADDED, 128), bf(2, 6, EXT, 128), bf(2, 6, EXT, 128), bf(2, 6, EXT, 128),
            fl(10, PADDED, 128),
            bf(2, 10, WP, 128), bf(2, 10, WP, 128), bf(10, WP, 128), bf(10, WP, 128),
            bf(HP, WP, 256), bf(HP, WP, 256), bf(HP, WP, 256),
            bf(1024, 256), bf(1024, 256), bf(1536, 256), bf(2048, 256),
            dma((8,)), dma((6,)), dma((2,)), dma((2, 10)), dma((2, 10)), dma((2,)), dma((2,)), dma((2,)), dma((2,)),
        ],
        compiler_params=pltpu.CompilerParams(
            collective_id=0, has_side_effects=True, vmem_limit_bytes=61 * 2**20
        ),
    )(
        plan, fields_in, in_proj, enc_conv, jnp.swapaxes(down_conv, 1, 2),
        mid_conv, up_proj, unite_conv,
    )
    return pl.pallas_call(
        project,
        name="project",
        out_shape=jax.ShapeDtypeStruct((2, VARS, H, W), BF),
        in_specs=[hbm, vmem],
        out_specs=hbm,
        scratch_shapes=[
            bf(2, HP, WP, 256), fl(2, VARS * H, W), bf(2, VARS, H, W), dma((2,)), dma((2,)),
        ],
        compiler_params=pltpu.CompilerParams(vmem_limit_bytes=61 * 2**20),
    )(merged, out_proj.T)


def solution(mesh):
    return jax.shard_map(
        shards,
        mesh=mesh,
        in_specs=(P("section", None, "lat", "lon"), P(), P(), P(), P(), P(), P(), P(), P()),
        out_specs=P("section", None, "lat", "lon"),
        check_vma=False,
    )
```

time: 53 us -> 38.4 us (0.72)
  the two profiles are of different devices: /device:TPU:6 before, /device:TPU:58 now
where the time goes in v2:
time: 38.4 us; the launch traced here: 38.2 us
  Pallas kernels  38.2 us (99%)
    pallas_call x1, Pallas kernels, shards(): pl.pallas_call(kernel, name='unet', out_shape=jax.ShapeDtypeStruct((2, HP...  34.6 us
    pallas_call x1, Pallas kernels, shards(): pl.pallas_call(project, name='project', out_shape=jax.ShapeDtypeStruct((2...  3.66 us

profile of v2, /device:TPU:58, one launch (start us, length us, event | category | flops | bytes accessed | tf_op | source)
XLA Modules:
  0.0 38.2 jit_solution(7346813503546420616)
XLA Ops:
  0.0 34.6 %unet.1.m_hbm = bf16[2,8,64,256]{3,2,1,0:T(8,128)(2,1)} custom-call(s32[4]{0:T(128)} %plan.1, bf16[2,96,16,128]{3,2,1,0:T(8,128)(2,1)} %x_hbm.1, bf16[64,96]{1,0:T(8,128)(2,1)} %win_hbm.1, bf16[9,64,64]{2,1,0:T(8,128)(2,1)} %wenc_hbm.1, bf16[9,64,128]{2,1,0:T(8,128)(2,1)} %bitcast.2, bf16[9,128,128]{2,1,0:T(8,128)(2,1)} %wmid_hbm.1, ...), custom_call_target="tpu_custom_call" | custom-call | tf_op jit(solution)/shard_map/unet/pallas_call | solution.py:591
  34.6 3.7 %project.1 = bf16[2,96,16,128]{3,2,1,0:T(8,128)(2,1)} custom-call(bf16[2,8,64,256]{3,2,1,0:T(8,128)(2,1)} %unet.1.m_hbm, bf16[64,96]{1,0:T(8,128)(2,1)} %bitcast.3), custom_call_target="tpu_custom_call" | custom-call | tf_op jit(solution)/shard_map/project/pallas_call | solution.py:622

commit v3 on v2

--- a/solution.py
+++ b/solution.py
@@ -11,6 +11,7 @@
 MESH = pl.DeviceIdType.MESH
 
 VARS, C0, C1 = 96, 64, 128
+COPIES = 8
 H, W = 16, 128
 HP, WP = H // 2, W // 2
 EXT = WP + 16
@@ -219,7 +220,13 @@
 
 
 def kept(value, keep):
-    return jnp.where(keep, value, 0.0)
+    return value if keep is None else jnp.where(keep, value, 0.0)
+
+
+def inside(row, first, last, above, below):
+    if isinstance(row, int):
+        return above if row < first else below if row > last else None
+    return ((row >= first) | above) & ((row <= last) | below)
 
 
 def encoder(above, below, ee, eb, we, fs, fp, qc, qs, group):
@@ -228,8 +235,7 @@
         y = rounded(gelu(nn(quads((ee, eb), first, group), we[...])))
         for p in range(group):
             ii = first + p
-            keep = ((ii >= 3) | above) & ((ii <= 10) | below)
-            v = kept(y[p * EXT : p * EXT + EXT], keep)
+            v = kept(y[p * EXT : p * EXT + EXT], inside(ii, 3, 10, above, below))
             v0, v1 = v[:, :128], v[:, 128:]
             fs[2 * ii, MID] = v0
             fs[2 * ii + 1, MID] = v1
@@ -264,8 +270,7 @@
         y = rounded(gelu(nn(row_quads((qs, qc), first, group_d), wd[...])))
         for p in range(group_d):
             k = first + p
-            keep = ((k >= 1) | above) & ((k <= 4) | below)
-            v = kept(y[p * EXT : p * EXT + EXT], keep)
+            v = kept(y[p * EXT : p * EXT + EXT], inside(k, 1, 4, above, below))
             fd[2 * k, MID] = v[:, :128]
             fd[2 * k + 1, MID] = v[:, 128:]
 
@@ -292,12 +297,8 @@
             k = first + p
             for dr in range(2):
                 v = y[p * EXT : p * EXT + EXT, dr * 128 : dr * 128 + 128]
-                v = v + fd[2 * k + 1 + dr, MID]
-                if dr == 0:
-                    keep = (k >= 1) | above
-                else:
-                    keep = (k <= 3) | below
-                rows.append(kept(v, keep).astype(BF))
+                keep = inside(2 * k + dr, 1, 8, above, below)
+                rows.append(kept(v + fd[2 * k + 1 + dr, MID], keep).astype(BF))
         z = rounded(nt(jnp.concatenate(rows, axis=0), up))
         for p in range(group_m):
             k = first + p
@@ -336,13 +337,38 @@
     return gelu(nn(jnp.concatenate(pieces, axis=1), wu[...])).astype(BF)
 
 
+def project_weights(wout_ref, both, gather):
+    w = nt(eye(VARS), wout_ref[...]).astype(BF)
+    zero = jnp.zeros((VARS, C0), BF)
+    both[...] = jnp.concatenate(
+        [jnp.concatenate([w, zero], axis=1), jnp.concatenate([zero, w], axis=1)], axis=0
+    )
+    i, j = grid_iota(256, 256)
+    gather[...] = one_hot((i // 64 % 2 == j // 128) & (j % 128 == 2 * (i % 64) + i // 128))
+
+
+def project(m_ref, both, gather, fo, out):
+    parts = []
+    for p in range(0, HP, 2):
+        m = [m_ref[p + k // 2][:, k % 2 * 128 : k % 2 * 128 + 128] for k in range(4)]
+        u = nt(both[...], jnp.concatenate(m, axis=0)).astype(BF)
+        for k in range(2):
+            lanes = slice(k * 128, k * 128 + 128)
+            parts.append(jnp.concatenate([u[:VARS, lanes], u[VARS:, lanes]], axis=1))
+    v = nn(jnp.concatenate(parts, axis=0), gather[...])
+    for h in range(H):
+        rows = v[h // 2 * VARS : h // 2 * VARS + VARS]
+        fo[pl.ds(h, VARS, stride=H), :] = rows[:, h % 2 * 128 : h % 2 * 128 + 128]
+    out[...] = fo[...].reshape(VARS, H, W).astype(BF)
+
+
 def kernel(
-    plan, x_hbm, win_hbm, wenc_hbm, wdown_hbm, wmid_hbm, wup_hbm, wun_hbm, out_hbm,
-    x_ref, win, wenc, wdown, wmid, wup, wun,
+    plan, x_hbm, win_hbm, wenc_hbm, wdown_hbm, wmid_hbm, wup_hbm, wun_hbm, wout_hbm, out_ref,
+    x_ref, win, wenc, wdown, wmid, wup, wun, wout,
     fx, send_a, main_b, recv_a, low, high, top, bot, left, right, ctl, ctr, cbl, cbr,
     f, ee, eb, fs, fp, qc, qs, fd, dm, dc, dp, fl, sc, sb, lc, lb,
-    merged_a, merged_b, recv_b, we, wd, wm, wu,
-    x_sem, w_sem, out_sem, halo_send, halo_recv, a_send, a_recv, b_send, b_recv,
+    merged_a, merged_b, recv_b, we, wd, wm, wu, both, gather,
+    x_sem, w_sem, halo_send, halo_recv, a_send, a_recv, b_send, b_recv,
 ):
     section, lat, lon = lax.axis_index("section"), lax.axis_index("lat"), lax.axis_index("lon")
     lats, lons = lax.axis_size("lat"), lax.axis_size("lon")
@@ -361,6 +387,7 @@
                 (wmid_hbm, wmid),
                 (wup_hbm, wup),
                 (wun_hbm, wun),
+                (wout_hbm, wout),
             )
         )
     ]
@@ -372,30 +399,30 @@
         )
         for n in range(8)
     ]
+    barrier = pltpu.get_barrier_semaphore()
+
+    def greet(device):
+        pl.semaphore_signal(barrier, inc=1, device_id=device, device_id_type=MESH)
+
+    greet(partner)
+    greet((section, lat, lt))
+    greet((section, lat, rt))
+
+    @pl.when(above)
+    def _():
+        for c in (lt, lon, rt):
+            greet((section, up, c))
+
+    @pl.when(below)
+    def _():
+        for c in (lt, lon, rt):
+            greet((section, dn, c))
+
     loads_w[0].start()
     for c in loads_x:
         c.start()
     for c in loads_w[1:]:
         c.start()
-
-    barrier = pltpu.get_barrier_semaphore()
-
-    def greet(device):
-        pl.semaphore_signal(barrier, inc=1, device_id=device, device_id_type=MESH)
-
-    greet(partner)
-    greet((section, lat, lt))
-    greet((section, lat, rt))
-
-    @pl.when(above)
-    def _():
-        for c in (lt, lon, rt):
-            greet((section, up, c))
-
-    @pl.when(below)
-    def _():
-        for c in (lt, lon, rt):
-            greet((section, dn, c))
 
     def copy_a(half):
         rows = pl.ds(8 * half, 8)
@@ -479,13 +506,13 @@
     for c in loads_x:
         c.wait()
     for half in range(2):
+        stem_rows(x_ref, index_a, win, fx, send_a, half)
+    for half in range(2):
         stem_rows(x_ref, 1 - index_a, win, fx, main_b, half)
     pl.semaphore_wait(barrier, greeted)
     for half in range(2):
+        copy_a(half).start()
         start_halo(0, main_b, half)
-    for half in range(2):
-        stem_rows(x_ref, index_a, win, fx, send_a, half)
-        copy_a(half).start()
 
     for n in range(2):
 
@@ -509,15 +536,16 @@
     prepare_down(wdown, wd)
     prepare_mid(wmid, wm)
     prepare_unite(wun, wu)
+    project_weights(wout, both, gather)
 
     finish_halo(0, main_b)
     widened(main_b, halo(0), f, ee, eb)
     copy_a(0).wait()
     start_halo(1, recv_a, 0)
     encoder(above, below, ee, eb, we, fs, fp, qc, qs, 14)
-    deepen(above, below, qc, qs, wd, fd, dm, dc, dp, 3)
     copy_a(1).wait()
     start_halo(1, recv_a, 1)
+    deepen(above, below, qc, qs, wd, fd, dm, dc, dp, 3)
     lift(above, below, dm, dc, dp, fd, wm, wup, fl, 5)
     join_operands(fs, fl, sc, sb, lc, lb)
 
@@ -531,9 +559,11 @@
     deepen(above, below, qc, qs, wd, fd, dm, dc, dp, 3)
     lift(above, below, dm, dc, dp, fd, wm, wup, fl, 5)
     join_operands(fs, fl, sc, sb, lc, lb)
-    merged_a[...] = unite(sc, sb, lc, lb, wu, 0, 8).reshape(8, WP, 256)
-    store_a = pltpu.make_async_copy(merged_a, out_hbm.at[section], out_sem.at[0])
-    store_a.start()
+    def unite_a(g):
+        merged_a[pl.ds(4 * g, 4)] = unite(sc, sb, lc, lb, wu, 4 * g, 4).reshape(4, WP, 256)
+
+    loop(2, 1, unite_a)
+    project(merged_a, both, gather, fx, out_ref.at[section])
 
     for half in range(2):
         copy_b(half).wait()
@@ -543,60 +573,41 @@
         merged_b[i] = jnp.where(stays, merged_b[i], recv_b[i])
 
     loop(HP, 4, choose)
-    store_b = pltpu.make_async_copy(merged_b, out_hbm.at[1 - section], out_sem.at[1])
-    store_b.start()
-    store_a.wait()
-    store_b.wait()
-
-
-def project(m_hbm, wout_ref, out_hbm, m_ref, fo, buf, load_sems, sems):
-    loads = [pltpu.make_async_copy(m_hbm.at[t], m_ref.at[t], load_sems.at[t]) for t in range(2)]
-    for load in loads:
-        load.start()
-    w = nt(eye(VARS), wout_ref[...]).astype(BF)
-    zero = jnp.zeros((VARS, C0), BF)
-    both = jnp.concatenate(
-        [jnp.concatenate([w, zero], axis=1), jnp.concatenate([zero, w], axis=1)], axis=0
-    )
-    i, j = grid_iota(256, 256)
-    gather = one_hot((i // 64 % 2 == j // 128) & (j % 128 == 2 * (i % 64) + i // 128))
-    copies = []
-    for t in range(2):
-        loads[t].wait()
-        parts = []
-        for p in range(0, HP, 2):
-            m = [m_ref[t, p + k // 2][:, k % 2 * 128 : k % 2 * 128 + 128] for k in range(4)]
-            u = nt(both, jnp.concatenate(m, axis=0)).astype(BF)
-            for k in range(2):
-                lanes = slice(k * 128, k * 128 + 128)
-                parts.append(jnp.concatenate([u[:VARS, lanes], u[VARS:, lanes]], axis=1))
-        v = nn(jnp.concatenate(parts, axis=0), gather)
-        for h in range(H):
-            rows = v[h // 2 * VARS : h // 2 * VARS + VARS]
-            fo[t, pl.ds(h, VARS, stride=H), :] = rows[:, h % 2 * 128 : h % 2 * 128 + 128]
-        buf[t] = fo[t].reshape(VARS, H, W).astype(BF)
-        copy = pltpu.make_async_copy(buf.at[t], out_hbm.at[t], sems.at[t])
-        copy.start()
-        copies.append(copy)
-    for copy in copies:
-        copy.wait()
+    project(merged_b, both, gather, fx, out_ref.at[1 - section])
+
+
+def hand_over(src, dst, buf, load_sems, store_sems):
+    rows = 2 * VARS // COPIES
+    parts = [(n * rows // VARS, pl.ds(n * rows % VARS, rows)) for n in range(COPIES)]
+    loads = [
+        pltpu.make_async_copy(src.at[p], buf.at[p], load_sems.at[n]) for n, p in enumerate(parts)
+    ]
+    stores = [
+        pltpu.make_async_copy(buf.at[p], dst.at[p], store_sems.at[n]) for n, p in enumerate(parts)
+    ]
+    for c in loads:
+        c.start()
+    for load, store in zip(loads, stores):
+        load.wait()
+        store.start()
+    for c in stores:
+        c.wait()
 
 
 def shards(fields_in, plan, in_proj, enc_conv, down_conv, mid_conv, up_proj, unite_conv, out_proj):
-    vmem = pl.BlockSpec(memory_space=pltpu.VMEM)
     hbm = pl.BlockSpec(memory_space=pltpu.HBM)
     dma = pltpu.SemaphoreType.DMA
     bf = lambda *s: pltpu.VMEM(s, BF)
     fl = lambda *s: pltpu.VMEM(s, F32)
-    merged = pl.pallas_call(
+    return pl.pallas_call(
         kernel,
         name="unet",
-        out_shape=jax.ShapeDtypeStruct((2, HP, WP, 256), BF),
-        in_specs=[pl.BlockSpec(memory_space=pltpu.SMEM)] + [hbm] * 7,
-        out_specs=hbm,
+        out_shape=pltpu.VMEM((2, VARS, H, W), BF),
+        in_specs=[pl.BlockSpec(memory_space=pltpu.SMEM)] + [hbm] * 8,
+        out_specs=pl.BlockSpec(memory_space=pltpu.VMEM),
         scratch_shapes=[
             bf(2, VARS, H, W), bf(C0, VARS), bf(9, C0, C0), bf(9, C0, C1), bf(9, C1, C1),
-            bf(C0, C1), bf(9, C0, C1),
+            bf(C0, C1), bf(9, C0, C1), bf(C0, VARS),
             fl(VARS * H, W),
             bf(H, WP, 128), bf(H, WP, 128), bf(H, WP, 128),
             bf(2, 8, 16, 128), bf(2, 8, 16, 128),
@@ -609,28 +620,16 @@
             fl(10, PADDED, 128),
             bf(2, 10, WP, 128), bf(2, 10, WP, 128), bf(10, WP, 128), bf(10, WP, 128),
             bf(HP, WP, 256), bf(HP, WP, 256), bf(HP, WP, 256),
-            bf(1024, 256), bf(1024, 256), bf(1536, 256), bf(2048, 256),
-            dma((8,)), dma((6,)), dma((2,)), dma((2, 10)), dma((2, 10)), dma((2,)), dma((2,)), dma((2,)), dma((2,)),
+            bf(1024, 256), bf(1024, 256), bf(1536, 256), bf(2048, 256), bf(2 * VARS, 128), bf(256, 256),
+            dma((8,)), dma((7,)), dma((2, 10)), dma((2, 10)), dma((2,)), dma((2,)), dma((2,)), dma((2,)),
         ],
         compiler_params=pltpu.CompilerParams(
             collective_id=0, has_side_effects=True, vmem_limit_bytes=61 * 2**20
         ),
     )(
         plan, fields_in, in_proj, enc_conv, jnp.swapaxes(down_conv, 1, 2),
-        mid_conv, up_proj, unite_conv,
+        mid_conv, up_proj, unite_conv, out_proj.T,
     )
-    return pl.pallas_call(
-        project,
-        name="project",
-        out_shape=jax.ShapeDtypeStruct((2, VARS, H, W), BF),
-        in_specs=[hbm, vmem],
-        out_specs=hbm,
-        scratch_shapes=[
-            bf(2, HP, WP, 256), fl(2, VARS * H, W), bf(2, VARS, H, W), dma((2,)), dma((2,)),
-        ],
-        compiler_params=pltpu.CompilerParams(vmem_limit_bytes=61 * 2**20),
-    )(merged, out_proj.T)
-
 
 def solution(mesh):
     return jax.shard_map(

time: 38.4 us -> 35.2 us (0.917)
  the two profiles are of different devices: /device:TPU:58 before, /device:TPU:62 now
where the time goes in v3:
time: 35.2 us; the launch traced here: 35 us
  Pallas kernels  34.1 us (97%)
  local copies, waits for them, and re-layouts  0.88 us (2%)
    pallas_call x1, Pallas kernels, shards(): pl.pallas_call(kernel, name='unet', out_shape=pltpu.VMEM((2, VARS, H, W),...  34.1 us
    unnamed x1, local copies, waits for them, and re-layouts  0.88 us

profile of v3, /device:TPU:62, one launch (start us, length us, event | category | flops | bytes accessed | tf_op | source)
XLA Modules:
  0.0 35.0 jit_solution(18306717793864842358)
XLA Ops:
  0.0 34.1 %unet.1 = bf16[2,96,16,128]{3,2,1,0:T(8,128)(2,1)S(1)} custom-call(s32[4]{0:T(128)} %plan.1, bf16[2,96,16,128]{3,2,1,0:T(8,128)(2,1)} %x_hbm.1, bf16[64,96]{1,0:T(8,128)(2,1)} %win_hbm.1, bf16[9,64,64]{2,1,0:T(8,128)(2,1)} %wenc_hbm.1, bf16[9,64,128]{2,1,0:T(8,128)(2,1)} %bitcast.2, bf16[9,128,128]{2,1,0:T(8,128)(2,1)} %wmid_hbm.1, bf16[64,128]{1,0:T(8,128)(2,1)} %wup_hbm.1, ...), custom_call_target="tpu_custom_call" | custom-call | tf_op jit(solution)/shard_map/unet/pallas_call | solution.py:602
  34.1 0.9 %copy.11 = bf16[2,96,16,128]{3,2,1,0:T(8,128)(2,1)} copy(bf16[2,96,16,128]{3,2,1,0:T(8,128)(2,1)S(1)} %unet.1) | data formatting | bytes 1572864

commit v4 on v3

--- a/solution.py
+++ b/solution.py
@@ -196,7 +196,7 @@
         f[1 + t, OWN] = top[t].astype(F32)
         f[24 + t, OWN] = bot[t].astype(F32)
 
-    loop(HP, 4, own)
+    loop(HP, 8, own)
     loop(4, 4, corner)
     loop(7, 7, rims)
     hi = upper_lanes(EXT)
@@ -207,7 +207,7 @@
             ee[par, q] = f[rr, MID].astype(BF)
             eb[par, q] = pltpu.roll(jnp.where(hi, f[rr, PREV], f[rr, NEXT]), 64, 1).astype(BF)
 
-    loop(16, 4, split)
+    loop(16, 8, split)
 
 
 def quads(refs, first, count):
@@ -283,7 +283,7 @@
             dc[par, q] = fd[dd, MID].astype(BF)
             dp[par, q] = fd[dd, NEXT].astype(BF)
 
-    loop(6, 3, split)
+    loop(6, 6, split)
 
 
 def lift(above, below, dm, dc, dp, fd, wm, wup_ref, fl, group_m):
@@ -320,7 +320,7 @@
                 jnp.where(hi, fs[idx, OWN_PREV], fs[idx, OWN_NEXT]), 64, 1
             ).astype(BF)
 
-    loop(10, 5, skip)
+    loop(10, 10, skip)
 
     def lift(m):
         lc[m] = fl[m, OWN].astype(BF)
@@ -367,7 +367,7 @@
     x_ref, win, wenc, wdown, wmid, wup, wun, wout,
     fx, send_a, main_b, recv_a, low, high, top, bot, left, right, ctl, ctr, cbl, cbr,
     f, ee, eb, fs, fp, qc, qs, fd, dm, dc, dp, fl, sc, sb, lc, lb,
-    merged_a, merged_b, recv_b, we, wd, wm, wu, both, gather,
+    merged, merged_b, recv_b, we, wd, wm, wu, both, gather,
     x_sem, w_sem, halo_send, halo_recv, a_send, a_recv, b_send, b_recv,
 ):
     section, lat, lon = lax.axis_index("section"), lax.axis_index("lat"), lax.axis_index("lon")
@@ -560,38 +560,24 @@
     lift(above, below, dm, dc, dp, fd, wm, wup, fl, 5)
     join_operands(fs, fl, sc, sb, lc, lb)
     def unite_a(g):
-        merged_a[pl.ds(4 * g, 4)] = unite(sc, sb, lc, lb, wu, 4 * g, 4).reshape(4, WP, 256)
+        merged[0, pl.ds(4 * g, 4)] = unite(sc, sb, lc, lb, wu, 4 * g, 4).reshape(4, WP, 256)
 
     loop(2, 1, unite_a)
-    project(merged_a, both, gather, fx, out_ref.at[section])
 
     for half in range(2):
         copy_b(half).wait()
     stays = jnp.where(section == 0, plan[1] < 2, plan[2] >= 2)
 
     def choose(i):
-        merged_b[i] = jnp.where(stays, merged_b[i], recv_b[i])
-
-    loop(HP, 4, choose)
-    project(merged_b, both, gather, fx, out_ref.at[1 - section])
-
-
-def hand_over(src, dst, buf, load_sems, store_sems):
-    rows = 2 * VARS // COPIES
-    parts = [(n * rows // VARS, pl.ds(n * rows % VARS, rows)) for n in range(COPIES)]
-    loads = [
-        pltpu.make_async_copy(src.at[p], buf.at[p], load_sems.at[n]) for n, p in enumerate(parts)
-    ]
-    stores = [
-        pltpu.make_async_copy(buf.at[p], dst.at[p], store_sems.at[n]) for n, p in enumerate(parts)
-    ]
-    for c in loads:
-        c.start()
-    for load, store in zip(loads, stores):
-        load.wait()
-        store.start()
-    for c in stores:
-        c.wait()
+        merged[1, i] = jnp.where(stays, merged_b[i], recv_b[i])
+
+    loop(HP, 8, choose)
+
+    def finish(n):
+        turn = section + n * (1 - 2 * section)
+        project(merged.at[n], both, gather, fx, out_ref.at[turn])
+
+    loop(2, 1, finish)
 
 
 def shards(fields_in, plan, in_proj, enc_conv, down_conv, mid_conv, up_proj, unite_conv, out_proj):
@@ -619,7 +605,7 @@
             fl(12, PADDED, 128), bf(2, 6, EXT, 128), bf(2, 6, EXT, 128), bf(2, 6, EXT, 128),
             fl(10, PADDED, 128),
             bf(2, 10, WP, 128), bf(2, 10, WP, 128), bf(10, WP, 128), bf(10, WP, 128),
-            bf(HP, WP, 256), bf(HP, WP, 256), bf(HP, WP, 256),
+            bf(2, HP, WP, 256), bf(HP, WP, 256), bf(HP, WP, 256),
             bf(1024, 256), bf(1024, 256), bf(1536, 256), bf(2048, 256), bf(2 * VARS, 128), bf(256, 256),
             dma((8,)), dma((7,)), dma((2, 10)), dma((2, 10)), dma((2,)), dma((2,)), dma((2,)), dma((2,)),
         ],

time: 35.2 us -> 34.7 us (0.986)
  the two profiles are of different devices: /device:TPU:62 before, /device:TPU:58 now
where the time goes in v4:
time: 34.7 us; the launch traced here: 34.5 us
  Pallas kernels  33.6 us (97%)
  local copies, waits for them, and re-layouts  0.88 us (3%)
    pallas_call x1, Pallas kernels, shards(): pl.pallas_call(kernel, name='unet', out_shape=pltpu.VMEM((2, VARS, H, W),...  33.6 us
    unnamed x1, local copies, waits for them, and re-layouts  0.88 us

profile of v4, /device:TPU:58, one launch (start us, length us, event | category | flops | bytes accessed | tf_op | source)
XLA Modules:
  0.0 34.5 jit_solution(16433630480016414297)
XLA Ops:
  0.0 33.6 %unet.1 = bf16[2,96,16,128]{3,2,1,0:T(8,128)(2,1)S(1)} custom-call(s32[4]{0:T(128)} %plan.1, bf16[2,96,16,128]{3,2,1,0:T(8,128)(2,1)} %x_hbm.1, bf16[64,96]{1,0:T(8,128)(2,1)} %win_hbm.1, bf16[9,64,64]{2,1,0:T(8,128)(2,1)} %wenc_hbm.1, bf16[9,64,128]{2,1,0:T(8,128)(2,1)} %bitcast.2, bf16[9,128,128]{2,1,0:T(8,128)(2,1)} %wmid_hbm.1, bf16[64,128]{1,0:T(8,128)(2,1)} %wup_hbm.1, ...), custom_call_target="tpu_custom_call" | custom-call | tf_op jit(solution)/shard_map/unet/pallas_call | solution.py:588
  33.6 0.9 %copy.11 = bf16[2,96,16,128]{3,2,1,0:T(8,128)(2,1)} copy(bf16[2,96,16,128]{3,2,1,0:T(8,128)(2,1)S(1)} %unet.1) | data formatting | bytes 1572864

commit v5 on v4

--- a/solution.py
+++ b/solution.py
@@ -173,7 +173,24 @@
     loop(4, 4, body)
 
 
-def widened(main, halo, f, ee, eb):
+def operands(f, ee, eb, q, first, count):
+    hi = upper_lanes(count)
+    at = slice(first, first + count)
+    for par in range(2):
+        row = f.at[2 * q + par]
+        prev, this, after = (row[8 + first + d : 8 + first + d + count] for d in (-1, 0, 1))
+        ee[par, q, at] = this.astype(BF)
+        eb[par, q, at] = pltpu.roll(jnp.where(hi, prev, after), 64, 1).astype(BF)
+
+
+def widen_inner(main, f, ee, eb):
+    for q in range(HP):
+        f[8 + 2 * q, OWN] = main[2 * q].astype(F32)
+        f[9 + 2 * q, OWN] = main[2 * q + 1].astype(F32)
+        operands(f, ee, eb, 4 + q, 16, EXT - 32)
+
+
+def widen_outer(halo, f, ee, eb):
     top, bot, left, right, ctl, ctr, cbl, cbr = halo
 
     def sides(q, at, lref, rref):
@@ -183,31 +200,19 @@
         f[at, 80:88] = rv[0:8]
         f[at + 1, 80:88] = rv[8:16]
 
-    def own(q):
+    for q in range(HP):
         sides(q, 8 + 2 * q, left, right)
-        f[8 + 2 * q, OWN] = main[2 * q].astype(F32)
-        f[9 + 2 * q, OWN] = main[2 * q + 1].astype(F32)
-
-    def corner(q):
+    for q in range(4):
         sides(q, 2 * q, ctl, ctr)
         sides(q, 24 + 2 * q, cbl, cbr)
-
-    def rims(t):
+    for t in range(7):
         f[1 + t, OWN] = top[t].astype(F32)
         f[24 + t, OWN] = bot[t].astype(F32)
-
-    loop(HP, 8, own)
-    loop(4, 4, corner)
-    loop(7, 7, rims)
-    hi = upper_lanes(EXT)
-
-    def split(q):
-        for par in range(2):
-            rr = 2 * q + par
-            ee[par, q] = f[rr, MID].astype(BF)
-            eb[par, q] = pltpu.roll(jnp.where(hi, f[rr, PREV], f[rr, NEXT]), 64, 1).astype(BF)
-
-    loop(16, 8, split)
+    for q in range(HP):
+        operands(f, ee, eb, 4 + q, 0, 16)
+        operands(f, ee, eb, 4 + q, EXT - 16, 16)
+    for q in (0, 1, 2, 3, 12, 13, 14, 15):
+        operands(f, ee, eb, q, 0, EXT)
 
 
 def quads(refs, first, count):
@@ -538,8 +543,9 @@
     prepare_unite(wun, wu)
     project_weights(wout, both, gather)
 
+    widen_inner(main_b, f, ee, eb)
     finish_halo(0, main_b)
-    widened(main_b, halo(0), f, ee, eb)
+    widen_outer(halo(0), f, ee, eb)
     copy_a(0).wait()
     start_halo(1, recv_a, 0)
     encoder(above, below, ee, eb, we, fs, fp, qc, qs, 14)
@@ -553,8 +559,9 @@
         merged_b[pl.ds(4 * half, 4)] = unite(sc, sb, lc, lb, wu, 4 * half, 4).reshape(4, WP, 256)
         copy_b(half).start()
 
+    widen_inner(recv_a, f, ee, eb)
     finish_halo(1, recv_a)
-    widened(recv_a, halo(1), f, ee, eb)
+    widen_outer(halo(1), f, ee, eb)
     encoder(above, below, ee, eb, we, fs, fp, qc, qs, 14)
     deepen(above, below, qc, qs, wd, fd, dm, dc, dp, 3)
     lift(above, below, dm, dc, dp, fd, wm, wup, fl, 5)

time: 34.7 us -> 34.8 us (level)
  no operation moved by 1% of the time
where the time goes in v5:
time: 34.8 us; the launch traced here: 34.6 us
  Pallas kernels  33.7 us (97%)
  local copies, waits for them, and re-layouts  0.88 us (3%)
    pallas_call x1, Pallas kernels, shards(): pl.pallas_call(kernel, name='unet', out_shape=pltpu.VMEM((2, VARS, H, W),...  33.7 us
    unnamed x1, local copies, waits for them, and re-layouts  0.88 us

profile of v5, /device:TPU:58, one launch (start us, length us, event | category | flops | bytes accessed | tf_op | source)
XLA Modules:
  0.0 34.6 jit_solution(14346272082081280515)
XLA Ops:
  0.0 33.7 %unet.1 = bf16[2,96,16,128]{3,2,1,0:T(8,128)(2,1)S(1)} custom-call(s32[4]{0:T(128)} %plan.1, bf16[2,96,16,128]{3,2,1,0:T(8,128)(2,1)} %x_hbm.1, bf16[64,96]{1,0:T(8,128)(2,1)} %win_hbm.1, bf16[9,64,64]{2,1,0:T(8,128)(2,1)} %wenc_hbm.1, bf16[9,64,128]{2,1,0:T(8,128)(2,1)} %bitcast.2, bf16[9,128,128]{2,1,0:T(8,128)(2,1)} %wmid_hbm.1, bf16[64,128]{1,0:T(8,128)(2,1)} %wup_hbm.1, ...), custom_call_target="tpu_custom_call" | custom-call | tf_op jit(solution)/shard_map/unet/pallas_call | solution.py:595
  33.7 0.9 %copy.11 = bf16[2,96,16,128]{3,2,1,0:T(8,128)(2,1)} copy(bf16[2,96,16,128]{3,2,1,0:T(8,128)(2,1)S(1)} %unet.1) | data formatting | bytes 1572864
